TPU v7x, 32 devices: a whole 2x2x4 slice. The times are simulated.
32 devices in a mesh: anim: 8 (over y, x, core), snp: 4 (over z).
Axes of the slice: x: 2, y: 2, z: 4, core: 2. Of those that a mesh axis runs over, the one named last changes fastest.
Arguments:
- core_geno: bfloat16 [12288, 49152], P('anim', 'snp'), may hold values from -10 to 10, as said below
- noncore_geno: bfloat16 [6144, 49152], P('anim', 'snp'), may hold values from -10 to 10, as said below
- core_inv: bfloat16 [12288, 12288], P('anim', 'snp'), may hold values from -0.0546875 to 0.0546875
- snp_effects: bfloat16 [256, 49152], P(None, 'snp'), may hold values from -0.02734375 to 0.02734375
- noncore_scale: float32 [6144], P('anim'), may hold values from 0.5 to 2
Outputs:
- noncore_out: float32 [256, 6144], P(None, 'anim')
- core_out: float32 [256, 12288], P(None, ('anim', 'snp'))
Inputs may be any that keep to these rules, and one draw needn't show every extreme that they name: `core_geno`: each column j is (c - 2 p_j) / sqrt(2 p_j (1 - p_j)) for codes c in 0, 1, 2 and a column frequency p_j shared with noncore_geno. `noncore_geno`: each column j is (c - 2 p_j) / sqrt(2 p_j (1 - p_j)) for codes c in 0, 1, 2 and a column frequency p_j shared with core_geno.
All inputs are finite; a program needn't handle non-finite values.
Results may differ from a plain program's by a relative error of at most 0.008.
Values may be sent and summed in bfloat16 or wider, within the bound.
No kernel may reach another device: no remote copies, remote signals or barrier semaphores. Data moves between devices by JAX's collectives and lax.ppermute only.
A program may use at most 128 MiB of HBM per device.

v0:
```python
import jax
import jax.numpy as jnp
from jax import lax
from jax.sharding import PartitionSpec as P

NSNP = 49152


def contract_last(left, right):
    return lax.dot_general(
        left, right, (((1,), (1,)), ((), ())), preferred_element_type=jnp.float32
    )


def core_columns(partial_value, base, tile_cols):
    snp_index = lax.axis_index("snp")
    summed = lax.psum(partial_value, "snp")
    value = summed if base is None else base.astype(jnp.float32) - summed
    block = value.astype(jnp.bfloat16)
    whole = lax.all_gather(block, "anim", axis=1, tiled=True)
    columns = lax.dynamic_slice_in_dim(whole, snp_index * tile_cols, tile_cols, 1)
    return (block, columns)


def marker_terms(partial_value):
    piece = lax.psum_scatter(partial_value, "anim", scatter_dimension=1, tiled=True)
    return lax.all_gather((piece / NSNP).astype(jnp.bfloat16), "anim", axis=1, tiled=True)


def local(core_geno, noncore_geno, core_inv, snp_effects, noncore_scale):
    tile_cols = core_inv.shape[1]
    core_partial = contract_last(snp_effects, core_geno)
    noncore_partial = contract_last(snp_effects, noncore_geno)
    core_vals, value_cols = core_columns(core_partial, None, tile_cols)
    noncore_vals = lax.psum(noncore_partial, "snp")
    weight_partial = contract_last(value_cols, core_inv)
    core_weights = lax.psum(weight_partial, "snp").astype(jnp.bfloat16)
    snp_core = marker_terms(jnp.dot(core_weights, core_geno, preferred_element_type=jnp.float32))
    predicted = lax.psum(contract_last(snp_core, noncore_geno), "snp")
    noncore_out = noncore_scale[None, :] * (noncore_vals - predicted)
    noncore_half = noncore_out.astype(jnp.bfloat16)
    snp_noncore = marker_terms(
        jnp.dot(noncore_half, noncore_geno, preferred_element_type=jnp.float32)
    )
    back_partial = contract_last(snp_noncore, core_geno)
    core_rest, rest_cols = core_columns(back_partial, core_vals, tile_cols)
    out_partial = contract_last(rest_cols, core_inv)
    core_out = lax.psum_scatter(out_partial, "snp", scatter_dimension=1, tiled=True)
    return (noncore_out, core_out)


def solution(mesh):
    return jax.shard_map(
        local,
        mesh=mesh,
        in_specs=(P("anim", "snp"), P("anim", "snp"), P("anim", "snp"), P(None, "snp"), P("anim")),
        out_specs=(P(None, "anim"), P(None, ("anim", "snp"))),
        check_vma=False,
    )
```

profile of v0, /device:TPU:0, one launch (start us, length us, event | category | flops | bytes accessed | tf_op | source)
XLA Modules:
  0.0 779.4 jit_solution(5825682007410808446)
XLA Ops:
  7.2 17.9 %fusion.11 = f32[256,1536]{1,0:T(8,128)S(1)} fusion(bf16[256,12288]{1,0:T(8,128)(2,1)} %param.8, bf16[1536,12288]{1,0:T(8,128)(2,1)} %param.5), kind=kOutput, calls=%fused_computation.15 | convolution fusion | flops 9663676416 | bytes 45613056 | tf_op jit(solution)/shard_map/dot_general | solution.py:10
  25.1 61.9 %all-reduce.9 = bf16[256,1536]{1,0:T(8,128)(2,1)} all-reduce(f32[256,1536]{1,0:T(8,128)S(1)} %fusion.11), channel_id=1, replica_groups=mesh['anim'=8,'snp'=4] {'snp'}, use_global_device_ids=true, to_apply=%region_1.0 | all-reduce | flops 393216 | bytes 2359296 | tf_op jit(solution)/shard_map/psum | solution.py:17
  87.1 44.5 %all-gather.5.cloned.1.call-done = bf16[256,12288]{1,0:T(8,128)(2,1)} async-done(((bf16[256,1536]{1,0:T(8,128)(2,1)}), bf16[256,12288]{1,0:T(8,128)(2,1)}) %all-gather.5.cloned.1.call-update) | async-done | bytes 6291472 | tf_op jit(solution)/shard_map/all_gather | solution.py:20
  131.7 5.7 fusion.2
  137.4 61.1 %all-reduce.10 = bf16[256,1536]{1,0:T(8,128)(2,1)S(1)} all-reduce(f32[256,1536]{1,0:T(8,128)S(1)} %fusion.2), channel_id=1, replica_groups=mesh['anim'=8,'snp'=4] {'snp'}, use_global_device_ids=true, to_apply=%region_2.0 | all-reduce | flops 393216 | bytes 2359296 | tf_op jit(solution)/shard_map/psum | solution.py:37
  198.5 19.4 %fusion.14 = f32[256,12288]{1,0:T(8,128)} fusion(bf16[256,1536]{1,0:T(8,128)(2,1)S(1)} %all-reduce.10, bf16[1536,12288]{1,0:T(8,128)(2,1)} %param.5), kind=kOutput, calls=%fused_computation.18 | convolution fusion | flops 9663676416 | bytes 51118080 | tf_op jit(solution)/shard_map/dot_general | solution.py:38
  218.0 90.4 %reduce-scatter.4.cloned.1.call-done = f32[256,1536]{1,0:T(8,128)} async-done(((f32[256,12288]{1,0:T(8,128)}), f32[256,1536]{1,0:T(8,128)}) %reduce-scatter.4.cloned.1.call-update) | async-done | bytes 1572880 | tf_op jit(solution)/shard_map/reduce_scatter | solution.py:26
  308.4 2.4 multiply_convert_fusion.1
  311.1 12.3 %fusion.10 = f32[256,768]{1,0:T(8,128)} fusion(bf16[256,12288]{1,0:T(8,128)(2,1)} %param.8, bf16[768,12288]{1,0:T(8,128)(2,1)} %param.6), kind=kOutput, calls=%fused_computation.14 | convolution fusion | flops 4831838208 | bytes 25952256 | tf_op jit(solution)/shard_map/dot_general | solution.py:10
  323.4 33.1 %all-gather.7.cloned.1.call-done = bf16[256,12288]{1,0:T(8,128)(2,1)} async-done(((bf16[256,1536]{1,0:T(8,128)(2,1)}), bf16[256,12288]{1,0:T(8,128)(2,1)}) %all-gather.7.cloned.1.call-update) | async-done | bytes 6291472 | tf_op jit(solution)/shard_map/all_gather | solution.py:27
  356.5 11.8 %fusion.12 = f32[256,768]{1,0:T(8,128)} fusion(bf16[256,12288]{1,0:T(8,128)(2,1)} %all-gather.7.cloned.1.call-done, bf16[768,12288]{1,0:T(8,128)(2,1)} %param.6), kind=kOutput, calls=%fused_computation.16 | convolution fusion | flops 4831838208 | bytes 25952256 | tf_op jit(solution)/shard_map/dot_general | solution.py:10
  368.4 69.6 %all-reduce.8.cloned.1.call-done = (f32[256,768]{1,0:T(8,128)}, f32[256,768]{1,0:T(8,128)}) async-done(((f32[256,768]{1,0:T(8,128)}, f32[256,768]{1,0:T(8,128)}), (f32[256,768]{1,0:T(8,128)}, f32[256,768]{1,0:T(8,128)})) %all-reduce.8.cloned.1.call-update) | async-done | bytes 1572880 | tf_op jit(solution)/shard_map/psum | solution.py:35
  438.0 1.5 subtract_multiply_fusion
  439.4 14.6 %fusion.6 = f32[256,12288]{1,0:T(8,128)} fusion(bf16[768,12288]{1,0:T(8,128)(2,1)} %param.6, f32[256,768]{1,0:T(8,128)S(1)} %subtract_multiply_fusion), kind=kOutput, calls=%fused_computation.10 | convolution fusion | flops 4832034816 | bytes 32243712 | tf_op jit(solution)/shard_map/dot_general | solution.py:43
  454.1 91.5 %reduce-scatter.6.cloned.1.call-done = f32[256,1536]{1,0:T(8,128)} async-done(((f32[256,12288]{1,0:T(8,128)}), f32[256,1536]{1,0:T(8,128)}) %reduce-scatter.6.cloned.1.call-update) | async-done | bytes 1572880 | tf_op jit(solution)/shard_map/reduce_scatter | solution.py:26
  545.6 2.4 multiply_convert_fusion
  548.2 45.6 %all-gather.9.cloned.1.call-done = bf16[256,12288]{1,0:T(8,128)(2,1)} async-done(((bf16[256,1536]{1,0:T(8,128)(2,1)}), bf16[256,12288]{1,0:T(8,128)(2,1)}) %all-gather.9.cloned.1.call-update) | async-done | bytes 6291472 | tf_op jit(solution)/shard_map/all_gather | solution.py:27
  593.8 19.1 %fusion.13 = f32[256,1536]{1,0:T(8,128)} fusion(bf16[256,12288]{1,0:T(8,128)(2,1)} %all-gather.9.cloned.1.call-done, bf16[1536,12288]{1,0:T(8,128)(2,1)} %param.5), kind=kOutput, calls=%fused_computation.17 | convolution fusion | flops 9663676416 | bytes 45613056 | tf_op jit(solution)/shard_map/dot_general | solution.py:10
  612.9 0.3 all-gather.11.cloned.1.call-start
  613.1 69.0 %all-reduce.6.cloned.1.call-done = f32[256,1536]{1,0:T(8,128)} async-done(((f32[256,1536]{1,0:T(8,128)}), f32[256,1536]{1,0:T(8,128)}) %all-reduce.6.cloned.1.call-update) | async-done | bytes 1572880 | tf_op jit(solution)/shard_map/psum | solution.py:17
  682.2 2.5 subtract_convert_fusion
  684.7 44.7 %all-gather.11.cloned.1.call-done = bf16[256,12288]{1,0:T(8,128)(2,1)} async-done(((bf16[256,1536]{1,0:T(8,128)(2,1)}), bf16[256,12288]{1,0:T(8,128)(2,1)}) %all-gather.11.cloned.1.call-update) | async-done | bytes 6291472 | tf_op jit(solution)/shard_map/all_gather | solution.py:20
  729.4 8.0 %fusion = f32[256,1536]{1,0:T(8,128)} fusion(bf16[1536,3072]{1,0:T(8,128)(2,1)} %param.7, bf16[256,12288]{1,0:T(8,128)(2,1)} %all-gather.11.cloned.1.call-done, s32[]{:T(128)S(6)} %select_n.4), kind=kOutput, calls=%fused_computation | convolution fusion | flops 2415919104 | bytes 12582916 | tf_op jit(solution)/shard_map/dot_general | solution.py:10
  737.4 35.4 %reduce-scatter.8.cloned.1.call-done = f32[256,384]{1,0:T(8,128)} async-done(((f32[256,1536]{1,0:T(8,128)}), f32[256,384]{1,0:T(8,128)}) %reduce-scatter.8.cloned.1.call-update) | async-done | bytes 393232 | tf_op jit(solution)/shard_map/reduce_scatter | solution.py:48
  (23 shorter events, 0.7 us)
Async XLA Ops:
  7.2 124.5 %all-gather.5.cloned.1.call-start = ((), (), s32[]{:S(2)}) async-start(), calls=%async_computation.3 | async-start | bytes 7077888 | tf_op jit(solution)/shard_map/all_gather | solution.py:20
  87.1 221.3 %reduce-scatter.4.cloned.1.call-start = ((), (), s32[]{:S(2)}) async-start(), calls=%async_computation.4 | async-start | bytes 14155776 | tf_op jit(solution)/shard_map/reduce_scatter | solution.py:26
  217.9 138.6 %all-gather.7.cloned.1.call-start = ((), (), s32[]{:S(2)}) async-start(), calls=%async_computation.5 | async-start | bytes 7077888 | tf_op jit(solution)/shard_map/all_gather | solution.py:27
  310.9 127.1 %all-reduce.8.cloned.1.call-start = ((), (), s32[]{:S(2)}) async-start(), calls=%async_computation.11 | async-start | bytes 3145728 | tf_op jit(solution)/shard_map/psum | solution.py:35
  323.4 114.6 %copy-start.2 = (f32[768]{0:T(1024)S(1)}, f32[768]{0:T(1024)}, u32[]{:S(2)}) copy-start(f32[768]{0:T(1024)} %param.9) | copy-start | bytes 9220
  368.3 177.3 %reduce-scatter.6.cloned.1.call-start = ((), (), s32[]{:S(2)}) async-start(), calls=%async_computation.6 | async-start | bytes 14155776 | tf_op jit(solution)/shard_map/reduce_scatter | solution.py:26
  439.4 14.6 %copy-start.1 = (f32[256,768]{1,0:T(8,128)}, f32[256,768]{1,0:T(8,128)S(1)}, u32[]{:S(2)}) copy-start(f32[256,768]{1,0:T(8,128)S(1)} %subtract_multiply_fusion) | copy-start | bytes 2359300
  454.0 139.7 %all-gather.9.cloned.1.call-start = ((), (), s32[]{:S(2)}) async-start(), calls=%async_computation.7 | async-start | bytes 7077888 | tf_op jit(solution)/shard_map/all_gather | solution.py:27
  548.1 134.1 %copy-start = (bf16[256,1536]{1,0:T(8,128)(2,1)S(1)}, bf16[256,1536]{1,0:T(8,128)(2,1)}, u32[]{:S(2)}) copy-start(bf16[256,1536]{1,0:T(8,128)(2,1)} %all-reduce.9) | copy-start | bytes 2359300
  548.1 134.0 %all-reduce.6.cloned.1.call-start = ((), (), s32[]{:S(2)}) async-start(), calls=%async_computation.8 | async-start | bytes 3145728 | tf_op jit(solution)/shard_map/psum | solution.py:17
  612.9 116.5 %all-gather.11.cloned.1.call-start = ((), (), s32[]{:S(2)}) async-start(), calls=%async_computation.9 | async-start | bytes 7077888 | tf_op jit(solution)/shard_map/all_gather | solution.py:20
  684.7 88.2 %reduce-scatter.8.cloned.1.call-start = ((), (), s32[]{:S(2)}) async-start(), calls=%async_computation.10 | async-start | bytes 1966080 | tf_op jit(solution)/shard_map/reduce_scatter | solution.py:48
Sparse Core Ops, SparseCore 0:
  87.2 44.4 all-gather.4
  218.1 90.3 reduce-scatter.3
  311.0 45.5 all-gather.6
  368.5 69.4 all-reduce.7
  454.2 91.4 reduce-scatter.5
  548.2 45.5 all-gather.8
  613.0 69.1 all-reduce.5
  684.8 44.5 all-gather.10
  737.5 35.2 reduce-scatter.7
where the time goes:
time: 780 us; the launch traced here: 779 us
  waiting for transfers between devices  524 us (67%)
  blocking collectives  123 us (16%)
  matrix products  109 us (14%)
  between operations  13.9 us (2%)
  other arithmetic  8.82 us (1%)
    reduce_scatter x2, waiting for transfers between devices, marker_terms(): lax.psum_scatter(partial_value, 'anim', scatter_dimension=1, tiled=True)  182 us
    all_gather x2, waiting for transfers between devices, core_columns(): whole = lax.all_gather(block, 'anim', axis=1, tiled=True)  89.2 us
    all_gather x2, waiting for transfers between devices, marker_terms(): lax.all_gather((piece / NSNP).astype(jnp.bfloat16), 'anim', axis=1, tiled...  78.8 us
    dot_general x6, matrix products, contract_last(): lax.dot_general(left, right, (((1,), (1,)), ((), ())), preferred_element_...  74.7 us
    psum x1, waiting for transfers between devices, local(): noncore_vals = lax.psum(noncore_partial, 'snp')  69.6 us
    psum x1, waiting for transfers between devices, core_columns(): summed = lax.psum(partial_value, 'snp')  69 us
    psum x1, blocking collectives, core_columns(): summed = lax.psum(partial_value, 'snp')  61.9 us
    psum x1, blocking collectives, local(): core_weights = lax.psum(weight_partial, 'snp').astype(jnp.bfloat16)  61.1 us
  transfers between devices with their start and end apart: 9, of which 9 were waited for; matrix products, arithmetic and copies ran while one was open for 2% of the time, Pallas kernels for 0%

commit v1 on v0

v1 whole, which is shorter than its diff:
```python
import functools

import jax
import jax.numpy as jnp
from jax import lax
from jax.sharding import PartitionSpec as P

F32, BF16 = jnp.float32, jnp.bfloat16
VALUE_CHUNKS = 2
MARKER_CHUNKS = 4


def contract_last(left, right):
    return lax.dot_general(
        left, right, (((1,), (1,)), ((), ())), preferred_element_type=F32
    )


def bits_of(count):
    return count.bit_length() - 1


def swap(x, axis, size, mask):
    return lax.ppermute(x, axis, [(i, i ^ mask) for i in range(size)])


def pick(x, index, axis=0):
    if isinstance(index, int):
        return lax.index_in_dim(x, index, axis, keepdims=False)
    return lax.dynamic_index_in_dim(x, index, axis, keepdims=False)


def add(x, y):
    return x.astype(F32) + y.astype(F32)


def bit_of(index, bit):
    return jnp.bitwise_and(jnp.right_shift(index, bit), 1)


def combine(items):
    return functools.reduce(jnp.add, [item.astype(F32) for item in items])


def reorder(items, index):
    for b in range(bits_of(len(items))):
        high = bit_of(index, b) == 1
        items = [jnp.where(high, items[i ^ (1 << b)], items[i]) for i in range(len(items))]
    return items


def scatter_snp(pieces, size):
    got = [swap(pieces[i], "snp", size, i) for i in reversed(range(1, size))]
    return combine([pieces[0]] + got)


def sum_snp(part, size, finish):
    s = lax.axis_index("snp")
    rows, cols = part.shape
    x = part.astype(BF16).reshape(size, rows // size, cols)
    mine = scatter_snp([pick(x, jnp.bitwise_xor(s, i)) for i in range(size)], size)
    mine = finish(mine).astype(BF16)
    items = [mine] + [swap(mine, "snp", size, i) for i in range(1, size)]
    return jnp.concatenate(reorder(items, s), axis=0)


def to_tile(part, na, ns, relative):
    a, s = lax.axis_index("anim"), lax.axis_index("snp")
    k = na // ns
    p = a // k
    x = part.reshape(ns, part.shape[0] // ns, part.shape[1])
    place = (lambda i: i) if relative else (lambda i: jnp.bitwise_xor(p, i))
    items = [pick(x, place(0))]
    items += [swap(pick(x, place(i)), "anim", na, i * k) for i in range(1, ns)]
    mine = scatter_snp(reorder(items, jnp.bitwise_xor(s, p)), ns).astype(BF16)
    rows = [None] * ns
    for i in reversed(range(1, ns)):
        rows[i] = swap(mine, "anim", na, i * k)
    rows[0] = mine
    blocks = [jnp.concatenate(rows, axis=0)]
    for b in range(bits_of(k)):
        high = bit_of(a, b) == 1
        other = [swap(block, "anim", na, 1 << b) for block in blocks]
        low = [jnp.where(high, o, m) for m, o in zip(blocks, other)]
        blocks = low + [jnp.where(high, m, o) for m, o in zip(blocks, other)]
    return blocks


def sum_anim(part, order, na, ns, finish):
    a = lax.axis_index("anim")
    nb, fixed = bits_of(na), bits_of(na // ns)
    rows, cols = part.shape
    x = part.astype(BF16).reshape([2] * nb + [rows // na, cols])
    axes = list(reversed(range(nb)))
    for n, b in enumerate(order):
        j = axes.index(b)
        bit = bit_of(a, b) if b < fixed else 0
        got = swap(pick(x, 1 - bit, j), "anim", na, 1 << b)
        x = add(pick(x, bit, j), got)
        if n < nb - 1:
            x = x.astype(BF16)
        axes.pop(j)
    x = finish(x).astype(BF16)
    for b in reversed(order):
        got = swap(x, "anim", na, 1 << b)
        axes = sorted(axes + [b], reverse=True)
        j = axes.index(b)
        if b < fixed:
            high = bit_of(a, b) == 1
            x = jnp.stack([jnp.where(high, got, x), jnp.where(high, x, got)], axis=j)
        else:
            x = jnp.stack([x, got], axis=j)
    return x.reshape(rows, cols)


def true_rows(x, na, ns):
    p = lax.axis_index("anim") // (na // ns)
    pieces = x.reshape(ns, x.shape[0] // ns, x.shape[1])
    return jnp.concatenate([pick(pieces, jnp.bitwise_xor(p, i)) for i in range(ns)], axis=0)


def local(na, ns, core_geno, noncore_geno, core_inv, snp_effects, noncore_scale):
    a = lax.axis_index("anim")
    reps, markers = snp_effects.shape
    total = markers * ns
    core_rows = core_geno.shape[0]
    vc = core_rows // VALUE_CHUNKS
    mc = markers // MARKER_CHUNKS
    nb = bits_of(na)
    orders = [[0] + list(range(1, nb)), [0] + list(reversed(range(1, nb)))]
    row_slices = [slice(i * vc, (i + 1) * vc) for i in range(VALUE_CHUNKS)]
    col_slices = [slice(i * mc, (i + 1) * mc) for i in range(MARKER_CHUNKS)]
    own_effects = pick(snp_effects.reshape(na, reps // na, markers), a)

    def tile_of(parts, relative):
        blocks = [to_tile(part.astype(BF16), na, ns, relative) for part in parts]
        return jnp.concatenate(
            [blocks[c][q] for q in range(na // ns) for c in range(VALUE_CHUNKS)], axis=1
        )

    def less(cols, x):
        return own_effects[:, cols].astype(F32) - x / total

    values = tile_of([contract_last(snp_effects, core_geno[rows]) for rows in row_slices], False)
    weights = jnp.concatenate(
        [sum_snp(contract_last(values, core_inv[rows]), ns, lambda x: x) for rows in row_slices],
        axis=1,
    )
    predicted = 0.0
    for n, cols in enumerate(col_slices):
        part = jnp.dot(weights, core_geno[:, cols], preferred_element_type=F32)
        rest = sum_anim(part, orders[n % 2], na, ns, functools.partial(less, cols))
        predicted = predicted + contract_last(rest, noncore_geno[:, cols])
    half = sum_snp(predicted, ns, lambda x: noncore_scale[None, :] * x)
    rests = []
    for n, cols in enumerate(col_slices):
        part = jnp.dot(half, noncore_geno[:, cols], preferred_element_type=F32)
        rests.append(sum_anim(part, orders[n % 2], na, ns, functools.partial(less, cols)))
    parts = []
    for rows in row_slices:
        terms = [contract_last(rest, core_geno[rows, cols]) for rest, cols in zip(rests, col_slices)]
        parts.append(functools.reduce(jnp.add, terms))
    core_rest = tile_of(parts, True)
    out = contract_last(core_rest, core_inv)
    core_out = scatter_snp(reorder(jnp.split(out.astype(BF16), ns, axis=1), lax.axis_index("snp")), ns)
    return true_rows(half, na, ns).astype(F32), true_rows(core_out, na, ns)


def solution(mesh):
    return jax.shard_map(
        functools.partial(local, mesh.shape["anim"], mesh.shape["snp"]),
        mesh=mesh,
        in_specs=(P("anim", "snp"), P("anim", "snp"), P("anim", "snp"), P(None, "snp"), P("anim")),
        out_specs=(P(None, "anim"), P(None, ("anim", "snp"))),
        check_vma=False,
    )
```

time: 780 us -> 388 us (0.50)
  waiting for transfers between devices: 524 us -> 151 us
  blocking collectives: 123 us -> 0 us
  starting transfers between devices: 0.78 us -> 117 us
  between operations: 13.9 us -> 2.24 us
  matrix products: 109 us -> 98.1 us
    reduce_scatter x3 -> x0, waiting for transfers between devices: 217 us -> none  [the longest x2 182 us: marker_terms(): lax.psum_scatter(partial_value, 'anim', scatter_dimension=1, tiled=True)]
    all_gather x4 -> x0, waiting for transfers between devices: 168 us -> none  [the longest x2 89.2 us: core_columns(): whole = lax.all_gather(block, 'anim', axis=1, tiled=True)]
    ppermute x0 -> x109, waiting for transfers between devices: none -> 151 us  [swap(): return lax.ppermute(x, axis, [(i, i ^ mask) for i in range(size)])]
    psum x2 -> x0, waiting for transfers between devices: 139 us -> none  [the longest x1 69.6 us: local(): noncore_vals = lax.psum(noncore_partial, 'snp')]
    psum x2 -> x0, blocking collectives: 123 us -> none  [the longest x1 61.9 us: core_columns(): summed = lax.psum(partial_value, 'snp')]
    ppermute x0 -> x109, starting transfers between devices: none -> 117 us  [swap(): return lax.ppermute(x, axis, [(i, i ^ mask) for i in range(size)])]
    dot_general x6 -> x17, matrix products: 74.7 us -> 66.9 us  [contract_last(): lax.dot_general(left, right, (((1,), (1,)), ((), ())), preferred_element_...]
    dot_general x2 -> x8, matrix products: 34 us -> 31.2 us  [the longest x4 25.7 us: local(): part = jnp.dot(weights, core_geno[:, cols], preferred_element_type=F32)]
  transfers between devices with their start and end apart: 9 -> 109, of which waited for: 9 -> 53; matrix products, arithmetic and copies ran while one was open for 2% -> 11% of each run, Pallas kernels for 0% -> 0%
where the time goes in v1:
time: 388 us; the launch traced here: 384 us
  waiting for transfers between devices  151 us (39%)
  starting transfers between devices  117 us (30%)
  matrix products  98.1 us (25%)
  other arithmetic  9.53 us (2%)
  local copies, waits for them, and re-layouts  6.49 us (2%)
    ppermute x109, waiting for transfers between devices, swap(): return lax.ppermute(x, axis, [(i, i ^ mask) for i in range(size)])  151 us
    ppermute x109, starting transfers between devices, swap(): return lax.ppermute(x, axis, [(i, i ^ mask) for i in range(size)])  117 us
    dot_general x17, matrix products, contract_last(): lax.dot_general(left, right, (((1,), (1,)), ((), ())), preferred_element_...  66.9 us
    dot_general x4, matrix products, local(): part = jnp.dot(weights, core_geno[:, cols], preferred_element_type=F32)  25.7 us
  transfers between devices with their start and end apart: 109, of which 53 were waited for; matrix products, arithmetic and copies ran while one was open for 11% of the time, Pallas kernels for 0%

profile of v1, /device:TPU:0, one launch (start us, length us, event | category | flops | bytes accessed | tf_op | source)
XLA Modules:
  0.0 384.2 jit_solution(2139983077008547427)
XLA Ops:
  0.7 12.5 %fusion.129 = bf16[256,768]{1,0:T(8,128)(2,1)S(1)} fusion(bf16[256,12288]{1,0:T(8,128)(2,1)} %param.8, bf16[1536,12288]{1,0:T(8,128)(2,1)} %param.5), kind=kOutput, calls=%fused_computation.103 | convolution fusion | flops 4832034816 | bytes 25559040 | tf_op jit(solution)/shard_map/dot_general | solution.py:14
  17.8 9.8 %fusion.132 = bf16[256,768]{1,0:T(8,128)(2,1)S(1)} fusion(bf16[256,12288]{1,0:T(8,128)(2,1)S(1)} %copy-done, bf16[1536,12288]{1,0:T(8,128)(2,1)} %param.5), kind=kOutput, calls=%fused_computation.104 | convolution fusion | flops 4832034816 | bytes 25559040 | tf_op jit(solution)/shard_map/dot_general | solution.py:14
  27.7 4.1 %collective-permute-start.3 = (bf16[64,768]{1,0:T(8,128)(2,1)S(1)}, bf16[64,768]{1,0:T(8,128)(2,1)S(1)}, u32[]{:S(2)}, u32[]{:S(2)}) collective-permute-start(bf16[64,768]{1,0:T(8,128)(2,1)S(1)} %get-tuple-element.51), channel_id=1, source_target_pairs={{0,3},{1,2},{2,1},{3,0},{4,7},{5,6},{6,5},{7,4},{8,11},{9,10},{10,... | collective-permute-start | bytes 294920 | tf_op jit(solution)/shard_map/ppermute | solution.py:24
  62.2 3.9 %fusion.126 = bf16[256,768]{1,0:T(8,128)(2,1)S(1)} fusion(bf16[1536,3072]{1,0:T(8,128)(2,1)} %param.7, bf16[256,768]{1,0:T(8,128)(2,1)S(1)} %get-tuple-element.44, bf16[256,768]{1,0:T(8,128)(2,1)S(1)} %get-tuple-element.42, bf16[256,768]{1,0:T(8,128)(2,1)S(1)} %get-tuple-element.43, bf16[256,768]{1,0:T(8,128)(2,1)S(1)} %get-tuple-element.41), kind=kOutput, calls=%fused_computation.102 | convolution fusion | flops 1214447616 | bytes 6684672 | tf_op jit(solution)/shard_map/dot_general | solution.py:14
  85.9 6.3 %collective-permute-done.21 = bf16[64,768]{1,0:T(8,128)(2,1)S(1)} collective-permute-done((bf16[64,768]{1,0:T(8,128)(2,1)S(1)}, bf16[64,768]{1,0:T(8,128)(2,1)S(1)}, u32[]{:S(2)}, u32[]{:S(2)}) %collective-permute-start.21) | collective-permute-done | bytes 98336 | tf_op jit(solution)/shard_map/ppermute | solution.py:24
  97.7 5.4 %collective-permute-done.24 = bf16[64,768]{1,0:T(8,128)(2,1)S(1)} collective-permute-done((bf16[64,768]{1,0:T(8,128)(2,1)S(1)}, bf16[64,768]{1,0:T(8,128)(2,1)S(1)}, u32[]{:S(2)}, u32[]{:S(2)}) %collective-permute-start.24) | collective-permute-done | bytes 98336 | tf_op jit(solution)/shard_map/ppermute | solution.py:24
  103.1 6.4 %fusion.51 = bf16[256,3072]{1,0:T(8,128)(2,1)S(1)} fusion(bf16[1536,12288]{1,0:T(8,128)(2,1)} %param.5, bf16[64,768]{1,0:T(8,128)(2,1)S(1)} %get-tuple-element.104, bf16[64,768]{1,0:T(8,128)(2,1)S(1)} %get-tuple-element.103, bf16[64,768]{1,0:T(8,128)(2,1)S(1)} %get-tuple-element.102, bf16[64,768]{1,0:T(8,128)(2,1)S(1)} %get-tuple-element.101, ...), kind=kOutput, calls=%fused_computation.49 | convolution fusion | flops 2422996992 | bytes 11796480 | tf_op jit(solution)/shard_map/dot_general | solution.py:151
  109.5 6.4 %fusion.54 = bf16[256,3072]{1,0:T(8,128)(2,1)S(1)} fusion(bf16[1536,12288]{1,0:T(8,128)(2,1)} %param.5, bf16[64,768]{1,0:T(8,128)(2,1)S(1)} %get-tuple-element.104, bf16[64,768]{1,0:T(8,128)(2,1)S(1)} %get-tuple-element.103, bf16[64,768]{1,0:T(8,128)(2,1)S(1)} %get-tuple-element.102, bf16[64,768]{1,0:T(8,128)(2,1)S(1)} %get-tuple-element.101, ...), kind=kOutput, calls=%fused_computation.50 | convolution fusion | flops 2422996992 | bytes 11796480 | tf_op jit(solution)/shard_map/dot_general | solution.py:151
  115.9 6.4 %fusion.57 = bf16[256,3072]{1,0:T(8,128)(2,1)S(1)} fusion(bf16[1536,12288]{1,0:T(8,128)(2,1)} %param.5, bf16[64,768]{1,0:T(8,128)(2,1)S(1)} %get-tuple-element.104, bf16[64,768]{1,0:T(8,128)(2,1)S(1)} %get-tuple-element.103, bf16[64,768]{1,0:T(8,128)(2,1)S(1)} %get-tuple-element.102, bf16[64,768]{1,0:T(8,128)(2,1)S(1)} %get-tuple-element.101, ...), kind=kOutput, calls=%fused_computation.51 | convolution fusion | flops 2422996992 | bytes 11796480 | tf_op jit(solution)/shard_map/dot_general | solution.py:151
  122.3 6.6 %fusion.48 = bf16[256,3072]{1,0:T(8,128)(2,1)S(1)} fusion(bf16[1536,12288]{1,0:T(8,128)(2,1)} %param.5, bf16[64,768]{1,0:T(8,128)(2,1)S(1)} %get-tuple-element.104, bf16[64,768]{1,0:T(8,128)(2,1)S(1)} %get-tuple-element.103, bf16[64,768]{1,0:T(8,128)(2,1)S(1)} %get-tuple-element.102, bf16[64,768]{1,0:T(8,128)(2,1)S(1)} %get-tuple-element.101, ...), kind=kOutput, calls=%fused_computation.48 | convolution fusion | flops 2422996992 | bytes 11796480 | tf_op jit(solution)/shard_map/dot_general | solution.py:151
  136.9 6.6 %collective-permute-done.39 = bf16[2,32,3072]{2,1,0:T(8,128)(2,1)S(1)} collective-permute-done((bf16[2,32,3072]{2,1,0:T(8,128)(2,1)S(1)}, bf16[2,32,3072]{2,1,0:T(8,128)(2,1)S(1)}, u32[]{:S(2)}, u32[]{:S(2)}) %collective-permute-start.39) | collective-permute-done | bytes 393248 | tf_op jit(solution)/shard_map/ppermute | solution.py:24
  146.4 7.5 %collective-permute-done.33 = bf16[2,32,3072]{2,1,0:T(8,128)(2,1)S(1)} collective-permute-done((bf16[2,32,3072]{2,1,0:T(8,128)(2,1)S(1)}, bf16[2,32,3072]{2,1,0:T(8,128)(2,1)S(1)}, u32[]{:S(2)}, u32[]{:S(2)}) %collective-permute-start.33) | collective-permute-done | bytes 393248 | tf_op jit(solution)/shard_map/ppermute | solution.py:24
  175.8 6.8 %collective-permute-done.54 = bf16[2,32,3072]{2,1,0:T(8,128)(2,1)S(1)} collective-permute-done((bf16[2,32,3072]{2,1,0:T(8,128)(2,1)S(1)}, bf16[2,32,3072]{2,1,0:T(8,128)(2,1)S(1)}, u32[]{:S(2)}, u32[]{:S(2)}) %collective-permute-start.54) | collective-permute-done | bytes 393248 | tf_op jit(solution)/shard_map/ppermute | solution.py:24
  183.5 4.6 %collective-permute-done.42 = bf16[2,32,3072]{2,1,0:T(8,128)(2,1)S(1)} collective-permute-done((bf16[2,32,3072]{2,1,0:T(8,128)(2,1)S(1)}, bf16[2,32,3072]{2,1,0:T(8,128)(2,1)S(1)}, u32[]{:S(2)}, u32[]{:S(2)}) %collective-permute-start.42) | collective-permute-done | bytes 393248 | tf_op jit(solution)/shard_map/ppermute | solution.py:24
  207.9 4.3 %collective-permute-done.57 = bf16[64,768]{1,0:T(8,128)(2,1)S(1)} collective-permute-done((bf16[64,768]{1,0:T(8,128)(2,1)S(1)}, bf16[64,768]{1,0:T(8,128)(2,1)S(1)}, u32[]{:S(2)}, u32[]{:S(2)}) %collective-permute-start.57) | collective-permute-done | bytes 98336 | tf_op jit(solution)/shard_map/ppermute | solution.py:24
  218.5 4.8 %collective-permute-done.60 = bf16[64,768]{1,0:T(8,128)(2,1)S(1)} collective-permute-done((bf16[64,768]{1,0:T(8,128)(2,1)S(1)}, bf16[64,768]{1,0:T(8,128)(2,1)S(1)}, u32[]{:S(2)}, u32[]{:S(2)}) %collective-permute-start.60) | collective-permute-done | bytes 98336 | tf_op jit(solution)/shard_map/ppermute | solution.py:24
  235.9 7.0 %collective-permute-done.63 = bf16[2,32,3072]{2,1,0:T(8,128)(2,1)S(1)} collective-permute-done((bf16[2,32,3072]{2,1,0:T(8,128)(2,1)S(1)}, bf16[2,32,3072]{2,1,0:T(8,128)(2,1)S(1)}, u32[]{:S(2)}, u32[]{:S(2)}) %collective-permute-start.63) | collective-permute-done | bytes 393248 | tf_op jit(solution)/shard_map/ppermute | solution.py:24
  245.8 5.5 %collective-permute-done.75 = bf16[2,32,3072]{2,1,0:T(8,128)(2,1)S(1)} collective-permute-done((bf16[2,32,3072]{2,1,0:T(8,128)(2,1)S(1)}, bf16[2,32,3072]{2,1,0:T(8,128)(2,1)S(1)}, u32[]{:S(2)}, u32[]{:S(2)}) %collective-permute-start.75) | collective-permute-done | bytes 393248 | tf_op jit(solution)/shard_map/ppermute | solution.py:24
  275.1 6.9 %collective-permute-done.66 = bf16[2,32,3072]{2,1,0:T(8,128)(2,1)S(1)} collective-permute-done((bf16[2,32,3072]{2,1,0:T(8,128)(2,1)S(1)}, bf16[2,32,3072]{2,1,0:T(8,128)(2,1)S(1)}, u32[]{:S(2)}, u32[]{:S(2)}) %collective-permute-start.66) | collective-permute-done | bytes 393248 | tf_op jit(solution)/shard_map/ppermute | solution.py:24
  282.8 5.3 %collective-permute-done.72 = bf16[2,32,3072]{2,1,0:T(8,128)(2,1)S(1)} collective-permute-done((bf16[2,32,3072]{2,1,0:T(8,128)(2,1)S(1)}, bf16[2,32,3072]{2,1,0:T(8,128)(2,1)S(1)}, u32[]{:S(2)}, u32[]{:S(2)}) %collective-permute-start.72) | collective-permute-done | bytes 393248 | tf_op jit(solution)/shard_map/ppermute | solution.py:24
  291.0 4.2 %fusion.24 = f32[256,768]{1,0:T(8,128)S(1)} fusion(bf16[256,3072]{1,0:T(8,128)(2,1)S(1)} %bitcast.387, bf16[1536,12288]{1,0:T(8,128)(2,1)} %param.5), kind=kOutput, calls=%fused_computation.24 | convolution fusion | flops 1207959552 | bytes 7077888 | tf_op jit(solution)/shard_map/dot_general | solution.py:14
  314.9 3.9 %fusion.114 = bf16[256,768]{1,0:T(8,128)(2,1)S(1)} fusion(f32[256,768]{1,0:T(8,128)S(1)} %fusion.105, bf16[256,3072]{1,0:T(8,128)(2,1)S(1)} %bitcast.377, bf16[1536,12288]{1,0:T(8,128)(2,1)} %param.5), kind=kOutput, calls=%fused_computation.98 | convolution fusion | flops 1208352768 | bytes 7471104 | tf_op jit(solution)/shard_map/dot_general | solution.py:14
  369.8 4.3 %collective-permute-done.106 = bf16[256,384]{1,0:T(8,128)(2,1)S(1)} collective-permute-done((bf16[256,384]{1,0:T(8,128)(2,1)S(1)}, bf16[256,384]{1,0:T(8,128)(2,1)S(1)}, u32[]{:S(2)}, u32[]{:S(2)}) %collective-permute-start.106) | collective-permute-done | bytes 196640 | tf_op jit(solution)/shard_map/ppermute | solution.py:24
  374.1 8.8 %collective-permute-done.107 = bf16[256,384]{1,0:T(8,128)(2,1)S(1)} collective-permute-done((bf16[256,384]{1,0:T(8,128)(2,1)S(1)}, bf16[256,384]{1,0:T(8,128)(2,1)S(1)}, u32[]{:S(2)}, u32[]{:S(2)}) %collective-permute-start.107) | collective-permute-done | bytes 196640 | tf_op jit(solution)/shard_map/ppermute | solution.py:24
  (364 shorter events, 233.6 us)
Async XLA Ops:
  13.2 14.4 %collective-permute-start.2 = (bf16[64,768]{1,0:T(8,128)(2,1)S(1)}, bf16[64,768]{1,0:T(8,128)(2,1)S(1)}, u32[]{:S(2)}, u32[]{:S(2)}) collective-permute-start(bf16[64,768]{1,0:T(8,128)(2,1)S(1)} %get-tuple-element.108), channel_id=1, source_target_pairs={{0,8},{4,12},{8,0},{12,4},{16,24},{20,28},{24,16},{28,20},{1,9},{5... | collective-permute-start | bytes 294920 | tf_op jit(solution)/shard_map/ppermute | solution.py:24
  47.5 12.9 %collective-permute-start.9 = (bf16[256,768]{1,0:T(8,128)(2,1)S(1)}, bf16[256,768]{1,0:T(8,128)(2,1)S(1)}, u32[]{:S(2)}, u32[]{:S(2)}) collective-permute-start(bf16[256,768]{1,0:T(8,128)(2,1)S(1)} %pad_maximum_fusion.17), channel_id=1, source_target_pairs={{0,4},{4,0},{8,12},{12,8},{16,20},{20,16},{24,28},{28,24},{1,5},{5... | collective-permute-start | bytes 1179656 | tf_op jit(solution)/shard_map/ppermute | solution.py:24
  76.3 15.9 %collective-permute-start.21 = (bf16[64,768]{1,0:T(8,128)(2,1)S(1)}, bf16[64,768]{1,0:T(8,128)(2,1)S(1)}, u32[]{:S(2)}, u32[]{:S(2)}) collective-permute-start(bf16[64,768]{1,0:T(8,128)(2,1)S(1)} %get-tuple-element.100), channel_id=1, source_target_pairs={{0,2},{1,3},{2,0},{3,1},{4,6},{5,7},{6,4},{7,5},{8,10},{9,11},{10,... | collective-permute-start | bytes 294920 | tf_op jit(solution)/shard_map/ppermute | solution.py:24
  81.4 13.3 %collective-permute-start.31 = (bf16[64,768]{1,0:T(8,128)(2,1)S(1)}, bf16[64,768]{1,0:T(8,128)(2,1)S(1)}, u32[]{:S(2)}, u32[]{:S(2)}) collective-permute-start(bf16[64,768]{1,0:T(8,128)(2,1)S(1)} %fusion.165), channel_id=1, source_target_pairs={{0,1},{1,0},{2,3},{3,2},{4,5},{5,4},{6,7},{7,6},{8,9},{9,8},{10,11... | collective-permute-start | bytes 294920 | tf_op jit(solution)/shard_map/ppermute | solution.py:24
  81.5 15.2 %collective-permute-start.30 = (bf16[64,768]{1,0:T(8,128)(2,1)S(1)}, bf16[64,768]{1,0:T(8,128)(2,1)S(1)}, u32[]{:S(2)}, u32[]{:S(2)}) collective-permute-start(bf16[64,768]{1,0:T(8,128)(2,1)S(1)} %fusion.165), channel_id=1, source_target_pairs={{0,2},{1,3},{2,0},{3,1},{4,6},{5,7},{6,4},{7,5},{8,10},{9,11},{10,... | collective-permute-start | bytes 294920 | tf_op jit(solution)/shard_map/ppermute | solution.py:24
  84.1 12.7 %collective-permute-start.29 = (bf16[64,768]{1,0:T(8,128)(2,1)S(1)}, bf16[64,768]{1,0:T(8,128)(2,1)S(1)}, u32[]{:S(2)}, u32[]{:S(2)}) collective-permute-start(bf16[64,768]{1,0:T(8,128)(2,1)S(1)} %fusion.165), channel_id=1, source_target_pairs={{0,3},{1,2},{2,1},{3,0},{4,7},{5,6},{6,5},{7,4},{8,11},{9,10},{10,... | collective-permute-start | bytes 294920 | tf_op jit(solution)/shard_map/ppermute | solution.py:24
  134.3 19.6 %collective-permute-start.33 = (bf16[2,32,3072]{2,1,0:T(8,128)(2,1)S(1)}, bf16[2,32,3072]{2,1,0:T(8,128)(2,1)S(1)}, u32[]{:S(2)}, u32[]{:S(2)}) collective-permute-start(bf16[2,32,3072]{2,1,0:T(8,128)(2,1)S(1)} %slice_bitcast_fusion.14), channel_id=1, source_target_pairs={{0,8},{4,12},{8,0},{12,4},{16,24},{20,28},{24,16},{28,20},{1,9},{5... | collective-permute-start | bytes 1179656 | tf_op jit(solution)/shard_map/ppermute | solution.py:24
  136.0 18.8 %collective-permute-start.51 = (bf16[2,32,3072]{2,1,0:T(8,128)(2,1)S(1)}, bf16[2,32,3072]{2,1,0:T(8,128)(2,1)S(1)}, u32[]{:S(2)}, u32[]{:S(2)}) collective-permute-start(bf16[2,32,3072]{2,1,0:T(8,128)(2,1)S(1)} %slice_bitcast_fusion.8), channel_id=1, source_target_pairs={{0,16},{4,20},{8,24},{12,28},{16,0},{20,4},{24,8},{28,12},{1,17},{... | collective-permute-start | bytes 1179656 | tf_op jit(solution)/shard_map/ppermute | solution.py:24
  143.6 14.4 %collective-permute-start.40 = (bf16[32,3072]{1,0:T(8,128)(2,1)S(1)}, bf16[32,3072]{1,0:T(8,128)(2,1)S(1)}, u32[]{:S(2)}, u32[]{:S(2)}) collective-permute-start(bf16[32,3072]{1,0:T(8,128)(2,1)S(1)} %slice_bitcast_fusion.28), channel_id=1, source_target_pairs={{0,8},{4,12},{8,0},{12,4},{16,24},{20,28},{24,16},{28,20},{1,9},{5... | collective-permute-start | bytes 589832 | tf_op jit(solution)/shard_map/ppermute | solution.py:24
  169.5 13.1 %collective-permute-start.54 = (bf16[2,32,3072]{2,1,0:T(8,128)(2,1)S(1)}, bf16[2,32,3072]{2,1,0:T(8,128)(2,1)S(1)}, u32[]{:S(2)}, u32[]{:S(2)}) collective-permute-start(bf16[2,32,3072]{2,1,0:T(8,128)(2,1)S(1)} %get-tuple-element.87), channel_id=1, source_target_pairs={{0,16},{4,20},{8,24},{12,28},{16,0},{20,4},{24,8},{28,12},{1,17},{... | collective-permute-start | bytes 1179656 | tf_op jit(solution)/shard_map/ppermute | solution.py:24
  173.7 14.3 %collective-permute-start.42 = (bf16[2,32,3072]{2,1,0:T(8,128)(2,1)S(1)}, bf16[2,32,3072]{2,1,0:T(8,128)(2,1)S(1)}, u32[]{:S(2)}, u32[]{:S(2)}) collective-permute-start(bf16[2,32,3072]{2,1,0:T(8,128)(2,1)S(1)} %get-tuple-element.91), channel_id=1, source_target_pairs={{0,16},{4,20},{8,24},{12,28},{16,0},{20,4},{24,8},{28,12},{1,17},{... | collective-permute-start | bytes 1179656 | tf_op jit(solution)/shard_map/ppermute | solution.py:24
  175.0 13.3 %collective-permute-start.36 = (bf16[2,32,3072]{2,1,0:T(8,128)(2,1)S(1)}, bf16[2,32,3072]{2,1,0:T(8,128)(2,1)S(1)}, u32[]{:S(2)}, u32[]{:S(2)}) collective-permute-start(bf16[2,32,3072]{2,1,0:T(8,128)(2,1)S(1)} %get-tuple-element.89), channel_id=1, source_target_pairs={{0,8},{4,12},{8,0},{12,4},{16,24},{20,28},{24,16},{28,20},{1,9},{5... | collective-permute-start | bytes 1179656 | tf_op jit(solution)/shard_map/ppermute | solution.py:24
  234.0 17.3 %collective-permute-start.75 = (bf16[2,32,3072]{2,1,0:T(8,128)(2,1)S(1)}, bf16[2,32,3072]{2,1,0:T(8,128)(2,1)S(1)}, u32[]{:S(2)}, u32[]{:S(2)}) collective-permute-start(bf16[2,32,3072]{2,1,0:T(8,128)(2,1)S(1)} %slice_bitcast_fusion.2), channel_id=1, source_target_pairs={{0,8},{4,12},{8,0},{12,4},{16,24},{20,28},{24,16},{28,20},{1,9},{5... | collective-permute-start | bytes 1179656 | tf_op jit(solution)/shard_map/ppermute | solution.py:24
  234.9 18.4 %collective-permute-start.81 = (bf16[2,32,3072]{2,1,0:T(8,128)(2,1)S(1)}, bf16[2,32,3072]{2,1,0:T(8,128)(2,1)S(1)}, u32[]{:S(2)}, u32[]{:S(2)}) collective-permute-start(bf16[2,32,3072]{2,1,0:T(8,128)(2,1)S(1)} %slice_bitcast_fusion), channel_id=1, source_target_pairs={{0,16},{4,20},{8,24},{12,28},{16,0},{20,4},{24,8},{28,12},{1,17},{... | collective-permute-start | bytes 1179656 | tf_op jit(solution)/shard_map/ppermute | solution.py:24
  243.1 14.4 %collective-permute-start.64 = (bf16[32,3072]{1,0:T(8,128)(2,1)S(1)}, bf16[32,3072]{1,0:T(8,128)(2,1)S(1)}, u32[]{:S(2)}, u32[]{:S(2)}) collective-permute-start(bf16[32,3072]{1,0:T(8,128)(2,1)S(1)} %slice_bitcast_fusion.22), channel_id=1, source_target_pairs={{0,16},{4,20},{8,24},{12,28},{16,0},{20,4},{24,8},{28,12},{1,17},{... | collective-permute-start | bytes 589832 | tf_op jit(solution)/shard_map/ppermute | solution.py:24
  245.0 12.5 %collective-permute-start.70 = (bf16[32,3072]{1,0:T(8,128)(2,1)S(1)}, bf16[32,3072]{1,0:T(8,128)(2,1)S(1)}, u32[]{:S(2)}, u32[]{:S(2)}) collective-permute-start(bf16[32,3072]{1,0:T(8,128)(2,1)S(1)} %slice_bitcast_fusion.20), channel_id=1, source_target_pairs={{0,8},{4,12},{8,0},{12,4},{16,24},{20,28},{24,16},{28,20},{1,9},{5... | collective-permute-start | bytes 589832 | tf_op jit(solution)/shard_map/ppermute | solution.py:24
  268.8 13.4 %collective-permute-start.84 = (bf16[2,32,3072]{2,1,0:T(8,128)(2,1)S(1)}, bf16[2,32,3072]{2,1,0:T(8,128)(2,1)S(1)}, u32[]{:S(2)}, u32[]{:S(2)}) collective-permute-start(bf16[2,32,3072]{2,1,0:T(8,128)(2,1)S(1)} %get-tuple-element.68), channel_id=1, source_target_pairs={{0,16},{4,20},{8,24},{12,28},{16,0},{20,4},{24,8},{28,12},{1,17},{... | collective-permute-start | bytes 1179656 | tf_op jit(solution)/shard_map/ppermute | solution.py:24
  273.0 15.1 %collective-permute-start.72 = (bf16[2,32,3072]{2,1,0:T(8,128)(2,1)S(1)}, bf16[2,32,3072]{2,1,0:T(8,128)(2,1)S(1)}, u32[]{:S(2)}, u32[]{:S(2)}) collective-permute-start(bf16[2,32,3072]{2,1,0:T(8,128)(2,1)S(1)} %get-tuple-element.74), channel_id=1, source_target_pairs={{0,16},{4,20},{8,24},{12,28},{16,0},{20,4},{24,8},{28,12},{1,17},{... | collective-permute-start | bytes 1179656 | tf_op jit(solution)/shard_map/ppermute | solution.py:24
  274.1 14.2 %collective-permute-start.78 = (bf16[2,32,3072]{2,1,0:T(8,128)(2,1)S(1)}, bf16[2,32,3072]{2,1,0:T(8,128)(2,1)S(1)}, u32[]{:S(2)}, u32[]{:S(2)}) collective-permute-start(bf16[2,32,3072]{2,1,0:T(8,128)(2,1)S(1)} %get-tuple-element.70), channel_id=1, source_target_pairs={{0,8},{4,12},{8,0},{12,4},{16,24},{20,28},{24,16},{28,20},{1,9},{5... | collective-permute-start | bytes 1179656 | tf_op jit(solution)/shard_map/ppermute | solution.py:24
  282.3 24.2 %collective-permute-start.85 = (bf16[2,2,32,3072]{3,2,1,0:T(8,128)(2,1)S(1)}, bf16[2,2,32,3072]{3,2,1,0:T(8,128)(2,1)S(1)}, u32[]{:S(2)}, u32[]{:S(2)}) collective-permute-start(bf16[2,2,32,3072]{3,2,1,0:T(8,128)(2,1)S(1)} %pad_maximum_fusion.16), channel_id=1, source_target_pairs={{0,4},{4,0},{8,12},{12,8},{16,20},{20,16},{24,28},{28,24},{1,5},{5... | collective-permute-start | bytes 2359304 | tf_op jit(solution)/shard_map/ppermute | solution.py:24
  288.4 18.1 %collective-permute-start.79 = (bf16[2,2,32,3072]{3,2,1,0:T(8,128)(2,1)S(1)}, bf16[2,2,32,3072]{3,2,1,0:T(8,128)(2,1)S(1)}, u32[]{:S(2)}, u32[]{:S(2)}) collective-permute-start(bf16[2,2,32,3072]{3,2,1,0:T(8,128)(2,1)S(1)} %pad_maximum_fusion.15), channel_id=1, source_target_pairs={{0,4},{4,0},{8,12},{12,8},{16,20},{20,16},{24,28},{28,24},{1,5},{5... | collective-permute-start | bytes 2359304 | tf_op jit(solution)/shard_map/ppermute | solution.py:24
  346.2 13.6 %collective-permute-start.105 = (bf16[256,768]{1,0:T(8,128)(2,1)S(1)}, bf16[256,768]{1,0:T(8,128)(2,1)S(1)}, u32[]{:S(2)}, u32[]{:S(2)}) collective-permute-start(bf16[256,768]{1,0:T(8,128)(2,1)S(1)} %pad_maximum_fusion.29), channel_id=1, source_target_pairs={{0,4},{4,0},{8,12},{12,8},{16,20},{20,16},{24,28},{28,24},{1,5},{5... | collective-permute-start | bytes 1179656 | tf_op jit(solution)/shard_map/ppermute | solution.py:24
  366.1 16.9 %collective-permute-start.107 = (bf16[256,384]{1,0:T(8,128)(2,1)S(1)}, bf16[256,384]{1,0:T(8,128)(2,1)S(1)}, u32[]{:S(2)}, u32[]{:S(2)}) collective-permute-start(bf16[256,384]{1,0:T(8,128)(2,1)S(1)} %get-tuple-element.27), channel_id=1, source_target_pairs={{0,2},{1,3},{2,0},{3,1},{4,6},{5,7},{6,4},{7,5},{8,10},{9,11},{10,... | collective-permute-start | bytes 589832 | tf_op jit(solution)/shard_map/ppermute | solution.py:24
  366.1 16.9 %collective-permute-start.108 = (bf16[256,384]{1,0:T(8,128)(2,1)S(1)}, bf16[256,384]{1,0:T(8,128)(2,1)S(1)}, u32[]{:S(2)}, u32[]{:S(2)}) collective-permute-start(bf16[256,384]{1,0:T(8,128)(2,1)S(1)} %get-tuple-element.28), channel_id=1, source_target_pairs={{0,1},{1,0},{2,3},{3,2},{4,5},{5,4},{6,7},{7,6},{8,9},{9,8},{10,11... | collective-permute-start | bytes 589832 | tf_op jit(solution)/shard_map/ppermute | solution.py:24
  (96 other events, 857.2 us)

commit v2 on v1

--- a/solution.py
+++ b/solution.py
@@ -3,17 +3,33 @@
 import jax
 import jax.numpy as jnp
 from jax import lax
+from jax.experimental import pallas as pl
+from jax.experimental.pallas import tpu as pltpu
 from jax.sharding import PartitionSpec as P
 
 F32, BF16 = jnp.float32, jnp.bfloat16
 VALUE_CHUNKS = 2
-MARKER_CHUNKS = 4
+SNP_CORE_SHARES = (1, 1)
 
 
 def contract_last(left, right):
     return lax.dot_general(
         left, right, (((1,), (1,)), ((), ())), preferred_element_type=F32
     )
+
+
+def shares_of(count, shares):
+    edges = [count * sum(shares[:i]) // sum(shares) for i in range(len(shares) + 1)]
+    return [slice(low, high) for low, high in zip(edges, edges[1:])]
+
+
+def halves_of(cols):
+    middle = (cols.start + cols.stop) // 2
+    return slice(cols.start, middle), slice(middle, cols.stop)
+
+
+def after(x, earlier):
+    return lax.optimization_barrier((x, earlier))[0]
 
 
 def bits_of(count):
@@ -86,31 +102,117 @@
     return blocks
 
 
-def sum_anim(part, order, na, ns, finish):
+class Order:
+    def __init__(self):
+        self.last = None
+
+    def __call__(self, x):
+        if self.last is not None:
+            x = after(x, self.last)
+        self.last = x
+        return x
+
+
+def sum_anim(order, make, na, ns, finish):
     a = lax.axis_index("anim")
     nb, fixed = bits_of(na), bits_of(na // ns)
-    rows, cols = part.shape
-    x = part.astype(BF16).reshape([2] * nb + [rows // na, cols])
-    axes = list(reversed(range(nb)))
-    for n, b in enumerate(order):
-        j = axes.index(b)
-        bit = bit_of(a, b) if b < fixed else 0
-        got = swap(pick(x, 1 - bit, j), "anim", na, 1 << b)
-        x = add(pick(x, bit, j), got)
-        if n < nb - 1:
-            x = x.astype(BF16)
-        axes.pop(j)
-    x = finish(x).astype(BF16)
-    for b in reversed(order):
-        got = swap(x, "anim", na, 1 << b)
-        axes = sorted(axes + [b], reverse=True)
-        j = axes.index(b)
-        if b < fixed:
-            high = bit_of(a, b) == 1
-            x = jnp.stack([jnp.where(high, got, x), jnp.where(high, x, got)], axis=j)
-        else:
-            x = jnp.stack([x, got], axis=j)
-    return x.reshape(rows, cols)
+    bit = bit_of(a, 0) if fixed else 0
+    parts = make(order)
+    rows, cols = parts[0].shape
+    parts = [part.astype(BF16).reshape([2] * nb + [rows // na, cols]) for part in parts]
+    send = order(jnp.concatenate([pick(x, 1 - bit, nb - 1) for x in parts], axis=-1))
+    got = swap(send, "anim", na, 1)
+    yield None
+    got = order(got)
+    halves = [
+        add(pick(x, bit, nb - 1), got[..., i * cols : (i + 1) * cols]).astype(BF16)
+        for i, x in enumerate(parts)
+    ]
+    routes = [list(range(1, nb)), list(reversed(range(1, nb)))]
+    axes = [list(reversed(range(1, nb))) for _ in routes]
+    for n in range(nb - 1):
+        places = [axes[i].index(route[n]) for i, route in enumerate(routes)]
+        sends = [order(pick(half, 1, j)) for half, j in zip(halves, places)]
+        gots = [swap(send, "anim", na, 1 << route[n]) for send, route in zip(sends, routes)]
+        yield None
+        for i, j in enumerate(places):
+            halves[i] = add(pick(halves[i], 0, j), order(gots[i]))
+            if n < nb - 2:
+                halves[i] = halves[i].astype(BF16)
+            axes[i].pop(j)
+    halves = [finish(i, half).astype(BF16) for i, half in enumerate(halves)]
+    for n in reversed(range(nb - 1)):
+        halves = [order(half) for half in halves]
+        gots = [swap(half, "anim", na, 1 << route[n]) for half, route in zip(halves, routes)]
+        yield None
+        for i, route in enumerate(routes):
+            axes[i] = sorted(axes[i] + [route[n]], reverse=True)
+            j = axes[i].index(route[n])
+            halves[i] = jnp.stack([halves[i], order(gots[i])], axis=j)
+    x = order(jnp.concatenate(halves, axis=-1))
+    got = swap(x, "anim", na, 1)
+    yield None
+    got = order(got)
+    if fixed:
+        odd = bit_of(a, 0) == 1
+        x = jnp.stack([jnp.where(odd, got, x), jnp.where(odd, x, got)], axis=nb - 1)
+    else:
+        x = jnp.stack([x, got], axis=nb - 1)
+    yield x.reshape(rows, 2 * cols)
+
+
+def columns_of(tile, slices, earlier):
+    def kernel(tile_ref, earlier_ref, *refs):
+        outs, token_ref, sems = refs[: len(slices)], refs[-2], refs[-1]
+        copies = [
+            pltpu.make_async_copy(tile_ref.at[:, pl.ds(cols.start, cols.stop - cols.start)], out, sems.at[i])
+            for i, (cols, out) in enumerate(zip(slices, outs))
+        ]
+        for copy in copies:
+            copy.start()
+        token_ref[...] = jnp.zeros_like(token_ref)
+        for copy in copies:
+            copy.wait()
+
+    shape = lambda cols: jax.ShapeDtypeStruct((tile.shape[0], cols.stop - cols.start), tile.dtype)
+    return pl.pallas_call(
+        kernel,
+        in_specs=[pl.BlockSpec(memory_space=pl.ANY)] * 2,
+        out_specs=[pl.BlockSpec(memory_space=pl.ANY)] * len(slices)
+        + [pl.BlockSpec(memory_space=pltpu.VMEM)],
+        out_shape=[shape(cols) for cols in slices] + [jax.ShapeDtypeStruct((8, 128), F32)],
+        scratch_shapes=[pltpu.SemaphoreType.DMA((len(slices),))],
+        cost_estimate=pl.CostEstimate(
+            flops=0, bytes_accessed=tile.size * tile.dtype.itemsize, transcendentals=0
+        ),
+        compiler_params=pltpu.CompilerParams(vmem_limit_bytes=30 << 20),
+    )(tile, earlier)
+
+
+def run_pair(makers, lead, na, ns, finishes, use, aside=None):
+    order = Order()
+    sums = [sum_anim(order, make, na, ns, finish) for make, finish in zip(makers, finishes)]
+    uses = [None, None]
+
+    def step(i):
+        if uses[i] is not None:
+            return next(uses[i], True)
+        done = next(sums[i])
+        if done is not None:
+            uses[i] = use(order, i, done)
+            return step(i)
+        return False
+
+    for _ in range(lead):
+        step(0)
+    count = 0
+    while not step(1):
+        step(0)
+        count += 1
+        if count == 2 and aside is not None:
+            aside(order)
+    while not step(0):
+        pass
 
 
 def true_rows(x, na, ns):
@@ -125,11 +227,7 @@
     total = markers * ns
     core_rows = core_geno.shape[0]
     vc = core_rows // VALUE_CHUNKS
-    mc = markers // MARKER_CHUNKS
-    nb = bits_of(na)
-    orders = [[0] + list(range(1, nb)), [0] + list(reversed(range(1, nb)))]
     row_slices = [slice(i * vc, (i + 1) * vc) for i in range(VALUE_CHUNKS)]
-    col_slices = [slice(i * mc, (i + 1) * mc) for i in range(MARKER_CHUNKS)]
     own_effects = pick(snp_effects.reshape(na, reps // na, markers), a)
 
     def tile_of(parts, relative):
@@ -138,28 +236,70 @@
             [blocks[c][q] for q in range(na // ns) for c in range(VALUE_CHUNKS)], axis=1
         )
 
-    def less(cols, x):
-        return own_effects[:, cols].astype(F32) - x / total
+    def less(cols, i, x):
+        low = cols.start + i * x.shape[-1]
+        return own_effects[:, low : low + x.shape[-1]].astype(F32) - x / total
 
     values = tile_of([contract_last(snp_effects, core_geno[rows]) for rows in row_slices], False)
     weights = jnp.concatenate(
         [sum_snp(contract_last(values, core_inv[rows]), ns, lambda x: x) for rows in row_slices],
         axis=1,
     )
-    predicted = 0.0
-    for n, cols in enumerate(col_slices):
-        part = jnp.dot(weights, core_geno[:, cols], preferred_element_type=F32)
-        rest = sum_anim(part, orders[n % 2], na, ns, functools.partial(less, cols))
-        predicted = predicted + contract_last(rest, noncore_geno[:, cols])
-    half = sum_snp(predicted, ns, lambda x: noncore_scale[None, :] * x)
-    rests = []
-    for n, cols in enumerate(col_slices):
-        part = jnp.dot(half, noncore_geno[:, cols], preferred_element_type=F32)
-        rests.append(sum_anim(part, orders[n % 2], na, ns, functools.partial(less, cols)))
-    parts = []
-    for rows in row_slices:
-        terms = [contract_last(rest, core_geno[rows, cols]) for rest, cols in zip(rests, col_slices)]
-        parts.append(functools.reduce(jnp.add, terms))
+    weights = lax.optimization_barrier(weights)
+    weights = lax.optimization_barrier(weights)
+    total_of = lambda items: functools.reduce(jnp.add, items)
+    slices = shares_of(markers, SNP_CORE_SHARES)
+    predicted = []
+
+    def core_term(order, cols):
+        left = weights if order.last is None else after(weights, order.last)
+        return [
+            jnp.dot(left, core_geno[:, mine], preferred_element_type=F32) for mine in halves_of(cols)
+        ]
+
+    noncore_slices = [mine for cols in slices for mine in halves_of(cols)]
+    noncore_tiles = []
+
+    def bring(order):
+        *tiles, order.last = columns_of(noncore_geno, noncore_slices, order.last)
+        noncore_tiles.extend(tiles)
+
+    def use_core(order, n, rest):
+        for i, low in enumerate(jnp.split(rest, 2, axis=1)):
+            predicted.append(contract_last(low, noncore_tiles[2 * n + i]))
+            if n == 0:
+                predicted[-1] = order(predicted[-1])
+        yield True
+
+    run_pair(
+        [functools.partial(core_term, cols=cols) for cols in slices],
+        2, na, ns, [functools.partial(less, cols) for cols in slices], use_core, bring,
+    )
+    half = lax.optimization_barrier(
+        sum_snp(total_of(predicted), ns, lambda x: noncore_scale[None, :] * x)
+    )
+    other = slices
+    terms = [[] for _ in row_slices]
+
+    def noncore_term(order, n):
+        left = half if order.last is None else after(half, order.last)
+        return [
+            jnp.dot(left, tile, preferred_element_type=F32) for tile in noncore_tiles[2 * n : 2 * n + 2]
+        ]
+
+    def use_noncore(order, n, rest):
+        for term, rows in zip(terms, row_slices):
+            term.append(contract_last(rest, core_geno[rows, other[n]]))
+            if n == 0:
+                term[-1] = order(term[-1])
+                yield False
+        yield True
+
+    run_pair(
+        [functools.partial(noncore_term, n=n) for n in range(2)],
+        2, na, ns, [functools.partial(less, cols) for cols in other], use_noncore,
+    )
+    parts = [total_of(term) for term in terms]
     core_rest = tile_of(parts, True)
     out = contract_last(core_rest, core_inv)
     core_out = scatter_snp(reorder(jnp.split(out.astype(BF16), ns, axis=1), lax.axis_index("snp")), ns)

time: 388 us -> 384 us (0.990)
  Pallas kernels: 0 us -> 7.09 us
  waiting for transfers between devices: 151 us -> 145 us
  matrix products: 98.1 us -> 93.5 us
    pallas_call x0 -> x1, Pallas kernels: none -> 7.09 us  [columns_of(): pl.pallas_call(kernel, in_specs=[pl.BlockSpec(memory_space=pl.ANY)] * 2,...]
    ppermute x109 -> x101, waiting for transfers between devices: 151 us -> 145 us  [swap(): return lax.ppermute(x, axis, [(i, i ^ mask) for i in range(size)])]
    dot_general x17 -> x13, matrix products: 66.9 us -> 62.3 us  [contract_last(): lax.dot_general(left, right, (((1,), (1,)), ((), ())), preferred_element_...]
    ppermute x109 -> x101, starting transfers between devices: 117 us -> 115 us  [swap(): return lax.ppermute(x, axis, [(i, i ^ mask) for i in range(size)])]
  transfers between devices with their start and end apart: 109 -> 101, of which waited for: 53 -> 53; matrix products, arithmetic and copies ran while one was open for 11% -> 14% of each run, Pallas kernels for 0% -> 2%
where the time goes in v2:
time: 384 us; the launch traced here: 380 us
  waiting for transfers between devices  145 us (38%)
  starting transfers between devices  115 us (30%)
  matrix products  93.5 us (24%)
  other arithmetic  12.2 us (3%)
  Pallas kernels  7.09 us (2%)
  local copies, waits for them, and re-layouts  5.5 us (1%)
    ppermute x101, waiting for transfers between devices, swap(): return lax.ppermute(x, axis, [(i, i ^ mask) for i in range(size)])  145 us
    ppermute x101, starting transfers between devices, swap(): return lax.ppermute(x, axis, [(i, i ^ mask) for i in range(size)])  115 us
    dot_general x13, matrix products, contract_last(): lax.dot_general(left, right, (((1,), (1,)), ((), ())), preferred_element_...  62.3 us
    dot_general x4, matrix products, core_term(): jnp.dot(left, core_geno[:, mine], preferred_element_type=F32)  25.6 us
  transfers between devices with their start and end apart: 101, of which 53 were waited for; matrix products, arithmetic and copies ran while one was open for 14% of the time, Pallas kernels for 2%

profile of v2, /device:TPU:0, one launch (start us, length us, event | category | flops | bytes accessed | tf_op | source)
XLA Modules:
  0.0 380.0 jit_solution(10827239021232262647)
XLA Ops:
  0.7 12.5 %fusion.86 = bf16[256,768]{1,0:T(8,128)(2,1)S(1)} fusion(bf16[256,12288]{1,0:T(8,128)(2,1)} %param.8, bf16[1536,12288]{1,0:T(8,128)(2,1)} %param.5), kind=kOutput, calls=%fused_computation.94 | convolution fusion | flops 4832034816 | bytes 25559040 | tf_op jit(solution)/shard_map/dot_general | solution.py:16
  17.8 9.8 %fusion.89 = bf16[256,768]{1,0:T(8,128)(2,1)S(1)} fusion(bf16[256,12288]{1,0:T(8,128)(2,1)S(1)} %copy-done.2, bf16[1536,12288]{1,0:T(8,128)(2,1)} %param.5), kind=kOutput, calls=%fused_computation.95 | convolution fusion | flops 4832034816 | bytes 25559040 | tf_op jit(solution)/shard_map/dot_general | solution.py:16
  85.9 6.3 %collective-permute-done.21 = bf16[64,768]{1,0:T(8,128)(2,1)S(1)} collective-permute-done((bf16[64,768]{1,0:T(8,128)(2,1)S(1)}, bf16[64,768]{1,0:T(8,128)(2,1)S(1)}, u32[]{:S(2)}, u32[]{:S(2)}) %collective-permute-start.21) | collective-permute-done | bytes 98336 | tf_op jit(solution)/shard_map/ppermute | solution.py:40
  97.7 5.4 %collective-permute-done.24 = bf16[64,768]{1,0:T(8,128)(2,1)S(1)} collective-permute-done((bf16[64,768]{1,0:T(8,128)(2,1)S(1)}, bf16[64,768]{1,0:T(8,128)(2,1)S(1)}, u32[]{:S(2)}, u32[]{:S(2)}) %collective-permute-start.24) | collective-permute-done | bytes 98336 | tf_op jit(solution)/shard_map/ppermute | solution.py:40
  103.2 6.6 %fusion.27 = bf16[256,3072]{1,0:T(8,128)(2,1)S(1)} fusion(bf16[256,1536]{1,0:T(8,128)(2,1)S(1)} %maximum_maximum_fusion.4, bf16[1536,12288]{1,0:T(8,128)(2,1)} %param.5), kind=kOutput, calls=%fused_computation.25 | convolution fusion | flops 2416705536 | bytes 11796480 | tf_op jit(solution)/shard_map/dot_general | solution.py:257
  109.8 6.3 %fusion.24 = bf16[256,3072]{1,0:T(8,128)(2,1)S(1)} fusion(bf16[256,1536]{1,0:T(8,128)(2,1)S(1)} %maximum_maximum_fusion.4, bf16[1536,12288]{1,0:T(8,128)(2,1)} %param.5), kind=kOutput, calls=%fused_computation.24 | convolution fusion | flops 2416705536 | bytes 11796480 | tf_op jit(solution)/shard_map/dot_general | solution.py:257
  124.5 6.5 %fusion.33 = bf16[256,3072]{1,0:T(8,128)(2,1)S(1)} fusion(bf16[256,1536]{1,0:T(8,128)(2,1)S(1)} %copy-done.1, bf16[1536,12288]{1,0:T(8,128)(2,1)} %param.5), kind=kOutput, calls=%fused_computation.27 | convolution fusion | flops 2416705536 | bytes 11796480 | tf_op jit(solution)/shard_map/dot_general | solution.py:257
  130.9 6.3 %fusion.30 = bf16[256,3072]{1,0:T(8,128)(2,1)S(1)} fusion(bf16[256,1536]{1,0:T(8,128)(2,1)S(1)} %copy-done.1, bf16[1536,12288]{1,0:T(8,128)(2,1)} %param.5), kind=kOutput, calls=%fused_computation.26 | convolution fusion | flops 2416705536 | bytes 11796480 | tf_op jit(solution)/shard_map/dot_general | solution.py:257
  149.4 5.6 %collective-permute-done.40 = bf16[2,32,3072]{2,1,0:T(8,128)(2,1)S(1)} collective-permute-done((bf16[2,32,3072]{2,1,0:T(8,128)(2,1)S(1)}, bf16[2,32,3072]{2,1,0:T(8,128)(2,1)S(1)}, u32[]{:S(2)}, u32[]{:S(2)}) %collective-permute-start.40) | collective-permute-done | bytes 393248 | tf_op jit(solution)/shard_map/ppermute | solution.py:40
  164.5 6.7 %collective-permute-done.42 = bf16[2,32,3072]{2,1,0:T(8,128)(2,1)S(1)} collective-permute-done((bf16[2,32,3072]{2,1,0:T(8,128)(2,1)S(1)}, bf16[2,32,3072]{2,1,0:T(8,128)(2,1)S(1)}, u32[]{:S(2)}, u32[]{:S(2)}) %collective-permute-start.42) | collective-permute-done | bytes 393248 | tf_op jit(solution)/shard_map/ppermute | solution.py:40
  174.0 7.1 %shard_map.68 = (bf16[768,3072]{1,0:T(8,128)(2,1)S(1)}, bf16[768,3072]{1,0:T(8,128)(2,1)S(1)}, bf16[768,3072]{1,0:T(8,128)(2,1)S(1)}, bf16[768,3072]{1,0:T(8,128)(2,1)S(1)}, f32[8,128]{1,0:T(8,128)}) custom-call(bf16[768,12288]{1,0:T(8,128)(2,1)} %tile_ref.1, bf16[32,3072]{1,0:T(8,128)(2,1)S(1)} %get-tuple-element.108.earlier_ref), custom_call_target="tpu_custom_call" | custom-call | bytes 18874368 | tf_op jit(solution)/shard_map/pallas_call | solution.py:178
  186.4 5.7 %collective-permute-done.49 = bf16[2,32,3072]{2,1,0:T(8,128)(2,1)S(1)} collective-permute-done((bf16[2,32,3072]{2,1,0:T(8,128)(2,1)S(1)}, bf16[2,32,3072]{2,1,0:T(8,128)(2,1)S(1)}, u32[]{:S(2)}, u32[]{:S(2)}) %collective-permute-start.49) | collective-permute-done | bytes 393248 | tf_op jit(solution)/shard_map/ppermute | solution.py:40
  208.8 4.4 %collective-permute-done.53 = bf16[64,768]{1,0:T(8,128)(2,1)S(1)} collective-permute-done((bf16[64,768]{1,0:T(8,128)(2,1)S(1)}, bf16[64,768]{1,0:T(8,128)(2,1)S(1)}, u32[]{:S(2)}, u32[]{:S(2)}) %collective-permute-start.53) | collective-permute-done | bytes 98336 | tf_op jit(solution)/shard_map/ppermute | solution.py:40
  219.3 4.9 %collective-permute-done.56 = bf16[64,768]{1,0:T(8,128)(2,1)S(1)} collective-permute-done((bf16[64,768]{1,0:T(8,128)(2,1)S(1)}, bf16[64,768]{1,0:T(8,128)(2,1)S(1)}, u32[]{:S(2)}, u32[]{:S(2)}) %collective-permute-start.56) | collective-permute-done | bytes 98336 | tf_op jit(solution)/shard_map/ppermute | solution.py:40
  237.1 9.2 %collective-permute-done.59 = bf16[2,32,3072]{2,1,0:T(8,128)(2,1)S(1)} collective-permute-done((bf16[2,32,3072]{2,1,0:T(8,128)(2,1)S(1)}, bf16[2,32,3072]{2,1,0:T(8,128)(2,1)S(1)}, u32[]{:S(2)}, u32[]{:S(2)}) %collective-permute-start.59) | collective-permute-done | bytes 393248 | tf_op jit(solution)/shard_map/ppermute | solution.py:40
  257.8 6.2 %collective-permute-done.66 = bf16[2,32,3072]{2,1,0:T(8,128)(2,1)S(1)} collective-permute-done((bf16[2,32,3072]{2,1,0:T(8,128)(2,1)S(1)}, bf16[2,32,3072]{2,1,0:T(8,128)(2,1)S(1)}, u32[]{:S(2)}, u32[]{:S(2)}) %collective-permute-start.66) | collective-permute-done | bytes 393248 | tf_op jit(solution)/shard_map/ppermute | solution.py:40
  273.3 5.3 %collective-permute-done.68 = bf16[2,32,3072]{2,1,0:T(8,128)(2,1)S(1)} collective-permute-done((bf16[2,32,3072]{2,1,0:T(8,128)(2,1)S(1)}, bf16[2,32,3072]{2,1,0:T(8,128)(2,1)S(1)}, u32[]{:S(2)}, u32[]{:S(2)}) %collective-permute-start.68) | collective-permute-done | bytes 393248 | tf_op jit(solution)/shard_map/ppermute | solution.py:40
  280.8 5.3 %collective-permute-done.74 = bf16[32,3072]{1,0:T(8,128)(2,1)S(1)} collective-permute-done((bf16[32,3072]{1,0:T(8,128)(2,1)S(1)}, bf16[32,3072]{1,0:T(8,128)(2,1)S(1)}, u32[]{:S(2)}, u32[]{:S(2)}) %collective-permute-start.74) | collective-permute-done | bytes 196640 | tf_op jit(solution)/shard_map/ppermute | solution.py:40
  290.9 6.3 %fusion.10 = f32[256,768]{1,0:T(8,128)S(1)} fusion(bf16[256,6144]{1,0:T(8,128)(2,1)S(1)} %bitcast.359, bf16[1536,12288]{1,0:T(8,128)(2,1)} %param.5), kind=kOutput, calls=%fused_computation.10 | convolution fusion | flops 2415919104 | bytes 13369344 | tf_op jit(solution)/shard_map/dot_general | solution.py:16
  298.4 6.3 %fusion.8 = f32[256,768]{1,0:T(8,128)S(1)} fusion(bf16[256,6144]{1,0:T(8,128)(2,1)S(1)} %bitcast.360, bf16[1536,12288]{1,0:T(8,128)(2,1)} %param.5), kind=kOutput, calls=%fused_computation.8 | convolution fusion | flops 2415919104 | bytes 13369344 | tf_op jit(solution)/shard_map/dot_general | solution.py:16
  305.7 6.3 %fusion.74 = bf16[256,768]{1,0:T(8,128)(2,1)S(1)} fusion(f32[256,768]{1,0:T(8,128)S(1)} %fusion.10, bf16[256,6144]{1,0:T(8,128)(2,1)S(1)} %bitcast.357, bf16[1536,12288]{1,0:T(8,128)(2,1)} %param.5), kind=kOutput, calls=%fused_computation.90 | convolution fusion | flops 2416312320 | bytes 13762560 | tf_op jit(solution)/shard_map/dot_general | solution.py:16
  315.6 7.0 %fusion.71 = bf16[256,768]{1,0:T(8,128)(2,1)S(1)} fusion(f32[256,768]{1,0:T(8,128)S(1)} %fusion.8, bf16[256,6144]{1,0:T(8,128)(2,1)S(1)} %bitcast.358, bf16[1536,12288]{1,0:T(8,128)(2,1)} %param.5), kind=kOutput, calls=%fused_computation.89 | convolution fusion | flops 2416312320 | bytes 13762560 | tf_op jit(solution)/shard_map/dot_general | solution.py:16
  365.6 4.3 %collective-permute-done.98 = bf16[256,384]{1,0:T(8,128)(2,1)S(1)} collective-permute-done((bf16[256,384]{1,0:T(8,128)(2,1)S(1)}, bf16[256,384]{1,0:T(8,128)(2,1)S(1)}, u32[]{:S(2)}, u32[]{:S(2)}) %collective-permute-start.98) | collective-permute-done | bytes 196640 | tf_op jit(solution)/shard_map/ppermute | solution.py:40
  370.0 8.8 %collective-permute-done.99 = bf16[256,384]{1,0:T(8,128)(2,1)S(1)} collective-permute-done((bf16[256,384]{1,0:T(8,128)(2,1)S(1)}, bf16[256,384]{1,0:T(8,128)(2,1)S(1)}, u32[]{:S(2)}, u32[]{:S(2)}) %collective-permute-start.99) | collective-permute-done | bytes 196640 | tf_op jit(solution)/shard_map/ppermute | solution.py:40
  (328 shorter events, 218.6 us)
Async XLA Ops:
  13.2 14.4 %collective-permute-start.2 = (bf16[64,768]{1,0:T(8,128)(2,1)S(1)}, bf16[64,768]{1,0:T(8,128)(2,1)S(1)}, u32[]{:S(2)}, u32[]{:S(2)}) collective-permute-start(bf16[64,768]{1,0:T(8,128)(2,1)S(1)} %get-tuple-element.270), channel_id=1, source_target_pairs={{0,8},{4,12},{8,0},{12,4},{16,24},{20,28},{24,16},{28,20},{1,9},{5... | collective-permute-start | bytes 294920 | tf_op jit(solution)/shard_map/ppermute | solution.py:40
  16.2 11.4 %collective-permute-start.1 = (bf16[64,768]{1,0:T(8,128)(2,1)S(1)}, bf16[64,768]{1,0:T(8,128)(2,1)S(1)}, u32[]{:S(2)}, u32[]{:S(2)}) collective-permute-start(bf16[64,768]{1,0:T(8,128)(2,1)S(1)} %get-tuple-element.271), channel_id=1, source_target_pairs={{0,16},{4,20},{8,24},{12,28},{16,0},{20,4},{24,8},{28,12},{1,17},{... | collective-permute-start | bytes 294920 | tf_op jit(solution)/shard_map/ppermute | solution.py:40
  47.5 12.9 %collective-permute-start.9 = (bf16[256,768]{1,0:T(8,128)(2,1)S(1)}, bf16[256,768]{1,0:T(8,128)(2,1)S(1)}, u32[]{:S(2)}, u32[]{:S(2)}) collective-permute-start(bf16[256,768]{1,0:T(8,128)(2,1)S(1)} %pad_maximum_fusion.11), channel_id=1, source_target_pairs={{0,4},{4,0},{8,12},{12,8},{16,20},{20,16},{24,28},{28,24},{1,5},{5... | collective-permute-start | bytes 1179656 | tf_op jit(solution)/shard_map/ppermute | solution.py:40
  76.3 15.9 %collective-permute-start.21 = (bf16[64,768]{1,0:T(8,128)(2,1)S(1)}, bf16[64,768]{1,0:T(8,128)(2,1)S(1)}, u32[]{:S(2)}, u32[]{:S(2)}) collective-permute-start(bf16[64,768]{1,0:T(8,128)(2,1)S(1)} %get-tuple-element.262), channel_id=1, source_target_pairs={{0,2},{1,3},{2,0},{3,1},{4,6},{5,7},{6,4},{7,5},{8,10},{9,11},{10,... | collective-permute-start | bytes 294920 | tf_op jit(solution)/shard_map/ppermute | solution.py:40
  81.4 13.3 %collective-permute-start.31 = (bf16[64,768]{1,0:T(8,128)(2,1)S(1)}, bf16[64,768]{1,0:T(8,128)(2,1)S(1)}, u32[]{:S(2)}, u32[]{:S(2)}) collective-permute-start(bf16[64,768]{1,0:T(8,128)(2,1)S(1)} %fusion.122), channel_id=1, source_target_pairs={{0,1},{1,0},{2,3},{3,2},{4,5},{5,4},{6,7},{7,6},{8,9},{9,8},{10,11... | collective-permute-start | bytes 294920 | tf_op jit(solution)/shard_map/ppermute | solution.py:40
  81.5 15.2 %collective-permute-start.30 = (bf16[64,768]{1,0:T(8,128)(2,1)S(1)}, bf16[64,768]{1,0:T(8,128)(2,1)S(1)}, u32[]{:S(2)}, u32[]{:S(2)}) collective-permute-start(bf16[64,768]{1,0:T(8,128)(2,1)S(1)} %fusion.122), channel_id=1, source_target_pairs={{0,2},{1,3},{2,0},{3,1},{4,6},{5,7},{6,4},{7,5},{8,10},{9,11},{10,... | collective-permute-start | bytes 294920 | tf_op jit(solution)/shard_map/ppermute | solution.py:40
  84.1 12.7 %collective-permute-start.29 = (bf16[64,768]{1,0:T(8,128)(2,1)S(1)}, bf16[64,768]{1,0:T(8,128)(2,1)S(1)}, u32[]{:S(2)}, u32[]{:S(2)}) collective-permute-start(bf16[64,768]{1,0:T(8,128)(2,1)S(1)} %fusion.122), channel_id=1, source_target_pairs={{0,3},{1,2},{2,1},{3,0},{4,7},{5,6},{6,5},{7,4},{8,11},{9,10},{10,... | collective-permute-start | bytes 294920 | tf_op jit(solution)/shard_map/ppermute | solution.py:40
  122.3 15.4 %collective-permute-start.34 = (bf16[2,32,3072]{2,1,0:T(8,128)(2,1)S(1)}, bf16[2,32,3072]{2,1,0:T(8,128)(2,1)S(1)}, u32[]{:S(2)}, u32[]{:S(2)}) collective-permute-start(bf16[2,32,3072]{2,1,0:T(8,128)(2,1)S(1)} %slice_bitcast_fusion.13), channel_id=1, source_target_pairs={{0,16},{4,20},{8,24},{12,28},{16,0},{20,4},{24,8},{28,12},{1,17},{... | collective-permute-start | bytes 1179656 | tf_op jit(solution)/shard_map/ppermute | solution.py:40
  123.9 13.6 %collective-permute-start.33 = (bf16[2,32,3072]{2,1,0:T(8,128)(2,1)S(1)}, bf16[2,32,3072]{2,1,0:T(8,128)(2,1)S(1)}, u32[]{:S(2)}, u32[]{:S(2)}) collective-permute-start(bf16[2,32,3072]{2,1,0:T(8,128)(2,1)S(1)} %slice_bitcast_fusion.14), channel_id=1, source_target_pairs={{0,8},{4,12},{8,0},{12,4},{16,24},{20,28},{24,16},{28,20},{1,9},{5... | collective-permute-start | bytes 1179656 | tf_op jit(solution)/shard_map/ppermute | solution.py:40
  141.6 13.4 %collective-permute-start.40 = (bf16[2,32,3072]{2,1,0:T(8,128)(2,1)S(1)}, bf16[2,32,3072]{2,1,0:T(8,128)(2,1)S(1)}, u32[]{:S(2)}, u32[]{:S(2)}) collective-permute-start(bf16[2,32,3072]{2,1,0:T(8,128)(2,1)S(1)} %slice_bitcast_fusion.10), channel_id=1, source_target_pairs={{0,8},{4,12},{8,0},{12,4},{16,24},{20,28},{24,16},{28,20},{1,9},{5... | collective-permute-start | bytes 1179656 | tf_op jit(solution)/shard_map/ppermute | solution.py:40
  143.2 12.0 %collective-permute-start.39 = (bf16[2,32,3072]{2,1,0:T(8,128)(2,1)S(1)}, bf16[2,32,3072]{2,1,0:T(8,128)(2,1)S(1)}, u32[]{:S(2)}, u32[]{:S(2)}) collective-permute-start(bf16[2,32,3072]{2,1,0:T(8,128)(2,1)S(1)} %slice_bitcast_fusion.11), channel_id=1, source_target_pairs={{0,16},{4,20},{8,24},{12,28},{16,0},{20,4},{24,8},{28,12},{1,17},{... | collective-permute-start | bytes 1179656 | tf_op jit(solution)/shard_map/ppermute | solution.py:40
  146.8 12.6 %collective-permute-start.38 = (bf16[32,3072]{1,0:T(8,128)(2,1)S(1)}, bf16[32,3072]{1,0:T(8,128)(2,1)S(1)}, u32[]{:S(2)}, u32[]{:S(2)}) collective-permute-start(bf16[32,3072]{1,0:T(8,128)(2,1)S(1)} %get-tuple-element.103), channel_id=1, source_target_pairs={{0,16},{4,20},{8,24},{12,28},{16,0},{20,4},{24,8},{28,12},{1,17},{... | collective-permute-start | bytes 589832 | tf_op jit(solution)/shard_map/ppermute | solution.py:40
  147.9 11.4 %collective-permute-start.41 = (bf16[32,3072]{1,0:T(8,128)(2,1)S(1)}, bf16[32,3072]{1,0:T(8,128)(2,1)S(1)}, u32[]{:S(2)}, u32[]{:S(2)}) collective-permute-start(bf16[32,3072]{1,0:T(8,128)(2,1)S(1)} %get-tuple-element.108.earlier_ref), channel_id=1, source_target_pairs={{0,8},{4,12},{8,0},{12,4},{16,24},{20,28},{24,16},{28,20},{1,9},{5... | collective-permute-start | bytes 589832 | tf_op jit(solution)/shard_map/ppermute | solution.py:40
  159.4 11.7 %collective-permute-start.42 = (bf16[2,32,3072]{2,1,0:T(8,128)(2,1)S(1)}, bf16[2,32,3072]{2,1,0:T(8,128)(2,1)S(1)}, u32[]{:S(2)}, u32[]{:S(2)}) collective-permute-start(bf16[2,32,3072]{2,1,0:T(8,128)(2,1)S(1)} %pad_maximum_fusion.13), channel_id=1, source_target_pairs={{0,8},{4,12},{8,0},{12,4},{16,24},{20,28},{24,16},{28,20},{1,9},{5... | collective-permute-start | bytes 1179656 | tf_op jit(solution)/shard_map/ppermute | solution.py:40
  171.3 11.5 %collective-permute-start.46 = (bf16[2,2,32,6144]{3,2,1,0:T(8,128)(2,1)S(1)}, bf16[2,2,32,6144]{3,2,1,0:T(8,128)(2,1)S(1)}, u32[]{:S(2)}, u32[]{:S(2)}) collective-permute-start(bf16[2,2,32,6144]{3,2,1,0:T(8,128)(2,1)S(1)} %maximum_maximum_fusion), channel_id=1, source_target_pairs={{0,4},{4,0},{8,12},{12,8},{16,20},{20,16},{24,28},{28,24},{1,5},{5... | collective-permute-start | bytes 4718600 | tf_op jit(solution)/shard_map/ppermute | solution.py:40
  234.5 11.9 %collective-permute-start.60 = (bf16[2,32,3072]{2,1,0:T(8,128)(2,1)S(1)}, bf16[2,32,3072]{2,1,0:T(8,128)(2,1)S(1)}, u32[]{:S(2)}, u32[]{:S(2)}) collective-permute-start(bf16[2,32,3072]{2,1,0:T(8,128)(2,1)S(1)} %slice_bitcast_fusion.5), channel_id=1, source_target_pairs={{0,16},{4,20},{8,24},{12,28},{16,0},{20,4},{24,8},{28,12},{1,17},{... | collective-permute-start | bytes 1179656 | tf_op jit(solution)/shard_map/ppermute | solution.py:40
  237.0 12.3 %collective-permute-start.62 = (bf16[2,2,32,6144]{3,2,0,1:T(8,128)(2,1)S(1)}, bf16[2,2,32,6144]{3,2,0,1:T(8,128)(2,1)S(1)}, u32[]{:S(2)}, u32[]{:S(2)}) collective-permute-start(bf16[2,2,32,6144]{3,2,0,1:T(8,128)(2,1)S(1)} %pad_maximum_fusion.8), channel_id=1, source_target_pairs={{0,4},{4,0},{8,12},{12,8},{16,20},{20,16},{24,28},{28,24},{1,5},{5... | collective-permute-start | bytes 4718600 | tf_op jit(solution)/shard_map/ppermute | solution.py:40
  250.0 14.1 %collective-permute-start.66 = (bf16[2,32,3072]{2,1,0:T(8,128)(2,1)S(1)}, bf16[2,32,3072]{2,1,0:T(8,128)(2,1)S(1)}, u32[]{:S(2)}, u32[]{:S(2)}) collective-permute-start(bf16[2,32,3072]{2,1,0:T(8,128)(2,1)S(1)} %slice_bitcast_fusion.2), channel_id=1, source_target_pairs={{0,8},{4,12},{8,0},{12,4},{16,24},{20,28},{24,16},{28,20},{1,9},{5... | collective-permute-start | bytes 1179656 | tf_op jit(solution)/shard_map/ppermute | solution.py:40
  250.6 13.6 %collective-permute-start.65 = (bf16[2,32,3072]{2,1,0:T(8,128)(2,1)S(1)}, bf16[2,32,3072]{2,1,0:T(8,128)(2,1)S(1)}, u32[]{:S(2)}, u32[]{:S(2)}) collective-permute-start(bf16[2,32,3072]{2,1,0:T(8,128)(2,1)S(1)} %slice_bitcast_fusion.3), channel_id=1, source_target_pairs={{0,16},{4,20},{8,24},{12,28},{16,0},{20,4},{24,8},{28,12},{1,17},{... | collective-permute-start | bytes 1179656 | tf_op jit(solution)/shard_map/ppermute | solution.py:40
  255.8 11.0 %collective-permute-start.64 = (bf16[32,3072]{1,0:T(8,128)(2,1)S(1)}, bf16[32,3072]{1,0:T(8,128)(2,1)S(1)}, u32[]{:S(2)}, u32[]{:S(2)}) collective-permute-start(bf16[32,3072]{1,0:T(8,128)(2,1)S(1)} %get-tuple-element.148), channel_id=1, source_target_pairs={{0,16},{4,20},{8,24},{12,28},{16,0},{20,4},{24,8},{28,12},{1,17},{... | collective-permute-start | bytes 589832 | tf_op jit(solution)/shard_map/ppermute | solution.py:40
  256.7 11.6 %collective-permute-start.67 = (bf16[32,3072]{1,0:T(8,128)(2,1)S(1)}, bf16[32,3072]{1,0:T(8,128)(2,1)S(1)}, u32[]{:S(2)}, u32[]{:S(2)}) collective-permute-start(bf16[32,3072]{1,0:T(8,128)(2,1)S(1)} %get-tuple-element.149), channel_id=1, source_target_pairs={{0,8},{4,12},{8,0},{12,4},{16,24},{20,28},{24,16},{28,20},{1,9},{5... | collective-permute-start | bytes 589832 | tf_op jit(solution)/shard_map/ppermute | solution.py:40
  342.7 12.9 %collective-permute-start.87 = (bf16[256,768]{1,0:T(8,128)(2,1)S(1)}, bf16[256,768]{1,0:T(8,128)(2,1)S(1)}, u32[]{:S(2)}, u32[]{:S(2)}) collective-permute-start(bf16[256,768]{1,0:T(8,128)(2,1)S(1)} %pad_maximum_fusion.22), channel_id=1, source_target_pairs={{0,4},{4,0},{8,12},{12,8},{16,20},{20,16},{24,28},{28,24},{1,5},{5... | collective-permute-start | bytes 1179656 | tf_op jit(solution)/shard_map/ppermute | solution.py:40
  362.2 16.6 %collective-permute-start.99 = (bf16[256,384]{1,0:T(8,128)(2,1)S(1)}, bf16[256,384]{1,0:T(8,128)(2,1)S(1)}, u32[]{:S(2)}, u32[]{:S(2)}) collective-permute-start(bf16[256,384]{1,0:T(8,128)(2,1)S(1)} %get-tuple-element.205), channel_id=1, source_target_pairs={{0,2},{1,3},{2,0},{3,1},{4,6},{5,7},{6,4},{7,5},{8,10},{9,11},{10,... | collective-permute-start | bytes 589832 | tf_op jit(solution)/shard_map/ppermute | solution.py:40
  362.2 16.6 %collective-permute-start.100 = (bf16[256,384]{1,0:T(8,128)(2,1)S(1)}, bf16[256,384]{1,0:T(8,128)(2,1)S(1)}, u32[]{:S(2)}, u32[]{:S(2)}) collective-permute-start(bf16[256,384]{1,0:T(8,128)(2,1)S(1)} %get-tuple-element.206), channel_id=1, source_target_pairs={{0,1},{1,0},{2,3},{3,2},{4,5},{5,4},{6,7},{7,6},{8,9},{9,8},{10,11... | collective-permute-start | bytes 589832 | tf_op jit(solution)/shard_map/ppermute | solution.py:40
  (85 other events, 775.3 us)

commit v3 on v2

--- a/solution.py
+++ b/solution.py
@@ -253,6 +253,9 @@
 
     def core_term(order, cols):
         left = weights if order.last is None else after(weights, order.last)
+        if order.last is not None:
+            part = jnp.dot(left, core_geno[:, cols], preferred_element_type=F32)
+            return jnp.split(part.astype(BF16), 2, axis=1)
         return [
             jnp.dot(left, core_geno[:, mine], preferred_element_type=F32) for mine in halves_of(cols)
         ]
@@ -288,11 +291,13 @@
         ]
 
     def use_noncore(order, n, rest):
-        for term, rows in zip(terms, row_slices):
-            term.append(contract_last(rest, core_geno[rows, other[n]]))
-            if n == 0:
-                term[-1] = order(term[-1])
-                yield False
+        if n == 0:
+            whole = order(contract_last(rest, core_geno[:, other[0]]))
+            for term, rows in zip(terms, row_slices):
+                term.append(whole[:, rows])
+        else:
+            for term, rows in zip(terms, row_slices):
+                term.append(contract_last(rest, core_geno[rows, other[1]]))
         yield True
 
     run_pair(

time: 384 us -> 379 us (0.987)
  matrix products: 93.5 us -> 86.8 us
  waiting for transfers between devices: 145 us -> 149 us
    dot_general x4 -> x2, matrix products: 25.6 us -> 12.8 us  [core_term(): jnp.dot(left, core_geno[:, mine], preferred_element_type=F32)]
    dot_general x0 -> x1, matrix products: none -> 9.39 us  [core_term(): part = jnp.dot(left, core_geno[:, cols], preferred_element_type=F32)]
    ppermute x101, waiting for transfers between devices: 145 us -> 149 us  [swap(): return lax.ppermute(x, axis, [(i, i ^ mask) for i in range(size)])]
    dot_general x13 -> x12, matrix products: 62.3 us -> 58.6 us  [contract_last(): lax.dot_general(left, right, (((1,), (1,)), ((), ())), preferred_element_...]
  transfers between devices with their start and end apart: 101 -> 101, of which waited for: 53 -> 54; matrix products, arithmetic and copies ran while one was open for 14% -> 13% of each run, Pallas kernels for 2% -> 2%
where the time goes in v3:
time: 379 us; the launch traced here: 375 us
  waiting for transfers between devices  149 us (39%)
  starting transfers between devices  113 us (30%)
  matrix products  86.8 us (23%)
  other arithmetic  11.8 us (3%)
  Pallas kernels  7.09 us (2%)
  local copies, waits for them, and re-layouts  5.65 us (1%)
    ppermute x101, waiting for transfers between devices, swap(): return lax.ppermute(x, axis, [(i, i ^ mask) for i in range(size)])  149 us
    ppermute x101, starting transfers between devices, swap(): return lax.ppermute(x, axis, [(i, i ^ mask) for i in range(size)])  113 us
    dot_general x12, matrix products, contract_last(): lax.dot_general(left, right, (((1,), (1,)), ((), ())), preferred_element_...  58.6 us
    dot_general x2, matrix products, core_term(): jnp.dot(left, core_geno[:, mine], preferred_element_type=F32)  12.8 us
    dot_general x1, matrix products, core_term(): part = jnp.dot(left, core_geno[:, cols], preferred_element_type=F32)  9.39 us
  transfers between devices with their start and end apart: 101, of which 54 were waited for; matrix products, arithmetic and copies ran while one was open for 13% of the time, Pallas kernels for 2%

profile of v3, /device:TPU:0, one launch (start us, length us, event | category | flops | bytes accessed | tf_op | source)
XLA Modules:
  0.0 374.9 jit_solution(124683491809459240)
XLA Ops:
  0.7 12.5 %fusion.79 = bf16[256,768]{1,0:T(8,128)(2,1)S(1)} fusion(bf16[256,12288]{1,0:T(8,128)(2,1)} %param.8, bf16[1536,12288]{1,0:T(8,128)(2,1)} %param.5), kind=kOutput, calls=%fused_computation.89 | convolution fusion | flops 4832034816 | bytes 25559040 | tf_op jit(solution)/shard_map/dot_general | solution.py:16
  17.8 9.5 %fusion.82 = bf16[256,768]{1,0:T(8,128)(2,1)S(1)} fusion(bf16[256,12288]{1,0:T(8,128)(2,1)S(1)} %copy-done.2, bf16[1536,12288]{1,0:T(8,128)(2,1)} %param.5), kind=kOutput, calls=%fused_computation.90 | convolution fusion | flops 4832034816 | bytes 25559040 | tf_op jit(solution)/shard_map/dot_general | solution.py:16
  27.4 4.1 %collective-permute-start.3 = (bf16[64,768]{1,0:T(8,128)(2,1)S(1)}, bf16[64,768]{1,0:T(8,128)(2,1)S(1)}, u32[]{:S(2)}, u32[]{:S(2)}) collective-permute-start(bf16[64,768]{1,0:T(8,128)(2,1)S(1)} %get-tuple-element.229), channel_id=1, source_target_pairs={{0,3},{1,2},{2,1},{3,0},{4,7},{5,6},{6,5},{7,4},{8,11},{9,10},{10,... | collective-permute-start | bytes 294920 | tf_op jit(solution)/shard_map/ppermute | solution.py:40
  61.8 3.9 %fusion.76 = bf16[256,768]{1,0:T(8,128)(2,1)S(1)} fusion(bf16[1536,3072]{1,0:T(8,128)(2,1)} %param.7, bf16[256,768]{1,0:T(8,128)(2,1)S(1)} %get-tuple-element.222, bf16[256,768]{1,0:T(8,128)(2,1)S(1)} %get-tuple-element.220, bf16[256,768]{1,0:T(8,128)(2,1)S(1)} %get-tuple-element.221, bf16[256,768]{1,0:T(8,128)(2,1)S(1)} %get-tuple-element.219), kind=kOutput, calls=%fused_computation.88 | convolution fusion | flops 1214447616 | bytes 6684672 | tf_op jit(solution)/shard_map/dot_general | solution.py:16
  85.5 6.4 %collective-permute-done.21 = bf16[64,768]{1,0:T(8,128)(2,1)S(1)} collective-permute-done((bf16[64,768]{1,0:T(8,128)(2,1)S(1)}, bf16[64,768]{1,0:T(8,128)(2,1)S(1)}, u32[]{:S(2)}, u32[]{:S(2)}) %collective-permute-start.21) | collective-permute-done | bytes 98336 | tf_op jit(solution)/shard_map/ppermute | solution.py:40
  97.4 5.4 %collective-permute-done.24 = bf16[64,768]{1,0:T(8,128)(2,1)S(1)} collective-permute-done((bf16[64,768]{1,0:T(8,128)(2,1)S(1)}, bf16[64,768]{1,0:T(8,128)(2,1)S(1)}, u32[]{:S(2)}, u32[]{:S(2)}) %collective-permute-start.24) | collective-permute-done | bytes 98336 | tf_op jit(solution)/shard_map/ppermute | solution.py:40
  102.9 6.6 %fusion.26 = bf16[256,3072]{1,0:T(8,128)(2,1)S(1)} fusion(bf16[256,1536]{1,0:T(8,128)(2,1)S(1)} %maximum_maximum_fusion.4, bf16[1536,12288]{1,0:T(8,128)(2,1)} %param.5), kind=kOutput, calls=%fused_computation.22 | convolution fusion | flops 2416705536 | bytes 11796480 | tf_op jit(solution)/shard_map/dot_general | solution.py:260
  109.4 6.3 %fusion.23 = bf16[256,3072]{1,0:T(8,128)(2,1)S(1)} fusion(bf16[256,1536]{1,0:T(8,128)(2,1)S(1)} %maximum_maximum_fusion.4, bf16[1536,12288]{1,0:T(8,128)(2,1)} %param.5), kind=kOutput, calls=%fused_computation.21 | convolution fusion | flops 2416705536 | bytes 11796480 | tf_op jit(solution)/shard_map/dot_general | solution.py:260
  124.1 9.4 %fusion.16 = bf16[256,6144]{1,0:T(8,128)(2,1)S(1)} fusion(bf16[256,1536]{1,0:T(8,128)(2,1)S(1)} %copy-done.1, bf16[1536,12288]{1,0:T(8,128)(2,1)} %param.5), kind=kOutput, calls=%fused_computation.16 | convolution fusion | flops 4833411072 | bytes 22806528 | tf_op jit(solution)/shard_map/dot_general | solution.py:257
  146.0 5.6 %collective-permute-done.40 = bf16[2,32,3072]{2,1,0:T(8,128)(2,1)S(1)} collective-permute-done((bf16[2,32,3072]{2,1,0:T(8,128)(2,1)S(1)}, bf16[2,32,3072]{2,1,0:T(8,128)(2,1)S(1)}, u32[]{:S(2)}, u32[]{:S(2)}) %collective-permute-start.40) | collective-permute-done | bytes 393248 | tf_op jit(solution)/shard_map/ppermute | solution.py:40
  161.4 6.3 %collective-permute-done.42 = bf16[2,32,3072]{2,1,0:T(8,128)(2,1)S(1)} collective-permute-done((bf16[2,32,3072]{2,1,0:T(8,128)(2,1)S(1)}, bf16[2,32,3072]{2,1,0:T(8,128)(2,1)S(1)}, u32[]{:S(2)}, u32[]{:S(2)}) %collective-permute-start.42) | collective-permute-done | bytes 393248 | tf_op jit(solution)/shard_map/ppermute | solution.py:40
  170.5 7.1 %shard_map.68 = (bf16[768,3072]{1,0:T(8,128)(2,1)S(1)}, bf16[768,3072]{1,0:T(8,128)(2,1)S(1)}, bf16[768,3072]{1,0:T(8,128)(2,1)S(1)}, bf16[768,3072]{1,0:T(8,128)(2,1)S(1)}, f32[8,128]{1,0:T(8,128)}) custom-call(bf16[768,12288]{1,0:T(8,128)(2,1)} %tile_ref.1, bf16[32,3072]{1,0:T(8,128)(2,1)S(1)} %get-tuple-element.107.earlier_ref), custom_call_target="tpu_custom_call" | custom-call | bytes 18874368 | tf_op jit(solution)/shard_map/pallas_call | solution.py:178
  183.3 5.4 %collective-permute-done.49 = bf16[2,32,3072]{2,1,0:T(8,128)(2,1)S(1)} collective-permute-done((bf16[2,32,3072]{2,1,0:T(8,128)(2,1)S(1)}, bf16[2,32,3072]{2,1,0:T(8,128)(2,1)S(1)}, u32[]{:S(2)}, u32[]{:S(2)}) %collective-permute-start.49) | collective-permute-done | bytes 393248 | tf_op jit(solution)/shard_map/ppermute | solution.py:40
  205.2 4.4 %collective-permute-done.53 = bf16[64,768]{1,0:T(8,128)(2,1)S(1)} collective-permute-done((bf16[64,768]{1,0:T(8,128)(2,1)S(1)}, bf16[64,768]{1,0:T(8,128)(2,1)S(1)}, u32[]{:S(2)}, u32[]{:S(2)}) %collective-permute-start.53) | collective-permute-done | bytes 98336 | tf_op jit(solution)/shard_map/ppermute | solution.py:40
  215.7 4.9 %collective-permute-done.56 = bf16[64,768]{1,0:T(8,128)(2,1)S(1)} collective-permute-done((bf16[64,768]{1,0:T(8,128)(2,1)S(1)}, bf16[64,768]{1,0:T(8,128)(2,1)S(1)}, u32[]{:S(2)}, u32[]{:S(2)}) %collective-permute-start.56) | collective-permute-done | bytes 98336 | tf_op jit(solution)/shard_map/ppermute | solution.py:40
  233.8 9.2 %collective-permute-done.59 = bf16[2,32,3072]{2,1,0:T(8,128)(2,1)S(1)} collective-permute-done((bf16[2,32,3072]{2,1,0:T(8,128)(2,1)S(1)}, bf16[2,32,3072]{2,1,0:T(8,128)(2,1)S(1)}, u32[]{:S(2)}, u32[]{:S(2)}) %collective-permute-start.59) | collective-permute-done | bytes 393248 | tf_op jit(solution)/shard_map/ppermute | solution.py:40
  254.6 6.3 %collective-permute-done.66 = bf16[2,32,3072]{2,1,0:T(8,128)(2,1)S(1)} collective-permute-done((bf16[2,32,3072]{2,1,0:T(8,128)(2,1)S(1)}, bf16[2,32,3072]{2,1,0:T(8,128)(2,1)S(1)}, u32[]{:S(2)}, u32[]{:S(2)}) %collective-permute-start.66) | collective-permute-done | bytes 393248 | tf_op jit(solution)/shard_map/ppermute | solution.py:40
  270.0 5.4 %collective-permute-done.68 = bf16[2,32,3072]{2,1,0:T(8,128)(2,1)S(1)} collective-permute-done((bf16[2,32,3072]{2,1,0:T(8,128)(2,1)S(1)}, bf16[2,32,3072]{2,1,0:T(8,128)(2,1)S(1)}, u32[]{:S(2)}, u32[]{:S(2)}) %collective-permute-start.68) | collective-permute-done | bytes 393248 | tf_op jit(solution)/shard_map/ppermute | solution.py:40
  277.5 5.3 %collective-permute-done.74 = bf16[32,3072]{1,0:T(8,128)(2,1)S(1)} collective-permute-done((bf16[32,3072]{1,0:T(8,128)(2,1)S(1)}, bf16[32,3072]{1,0:T(8,128)(2,1)S(1)}, u32[]{:S(2)}, u32[]{:S(2)}) %collective-permute-start.74) | collective-permute-done | bytes 196640 | tf_op jit(solution)/shard_map/ppermute | solution.py:40
  287.2 9.3 %fusion = f32[256,1536]{1,0:T(8,128)S(1)} fusion(bf16[256,6144]{1,0:T(8,128)(2,1)S(1)} %bitcast.365, bf16[1536,12288]{1,0:T(8,128)(2,1)} %param.5), kind=kOutput, calls=%fused_computation | convolution fusion | flops 4831838208 | bytes 23592960 | tf_op jit(solution)/shard_map/dot_general | solution.py:16
  301.0 6.3 %fusion.67 = bf16[256,768]{1,0:T(8,128)(2,1)S(1)} fusion(bf16[256,6144]{1,0:T(8,128)(2,1)S(1)} %bitcast.359, bf16[1536,12288]{1,0:T(8,128)(2,1)} %param.5, f32[256,1536]{1,0:T(8,128)S(1)} %fusion), kind=kOutput, calls=%fused_computation.85 | convolution fusion | flops 2416312320 | bytes 13762560 | tf_op jit(solution)/shard_map/dot_general | solution.py:16
  310.9 6.9 %fusion.64 = bf16[256,768]{1,0:T(8,128)(2,1)S(1)} fusion(bf16[256,6144]{1,0:T(8,128)(2,1)S(1)} %bitcast.360, bf16[1536,12288]{1,0:T(8,128)(2,1)} %param.5, f32[256,1536]{1,0:T(8,128)S(1)} %fusion), kind=kOutput, calls=%fused_computation.84 | convolution fusion | flops 2416312320 | bytes 13762560 | tf_op jit(solution)/shard_map/dot_general | solution.py:16
  360.5 4.3 %collective-permute-done.98 = bf16[256,384]{1,0:T(8,128)(2,1)S(1)} collective-permute-done((bf16[256,384]{1,0:T(8,128)(2,1)S(1)}, bf16[256,384]{1,0:T(8,128)(2,1)S(1)}, u32[]{:S(2)}, u32[]{:S(2)}) %collective-permute-start.98) | collective-permute-done | bytes 196640 | tf_op jit(solution)/shard_map/ppermute | solution.py:40
  364.8 8.8 %collective-permute-done.99 = bf16[256,384]{1,0:T(8,128)(2,1)S(1)} collective-permute-done((bf16[256,384]{1,0:T(8,128)(2,1)S(1)}, bf16[256,384]{1,0:T(8,128)(2,1)S(1)}, u32[]{:S(2)}, u32[]{:S(2)}) %collective-permute-start.99) | collective-permute-done | bytes 196640 | tf_op jit(solution)/shard_map/ppermute | solution.py:40
  (327 shorter events, 213.3 us)
Async XLA Ops:
  13.2 14.1 %collective-permute-start.2 = (bf16[64,768]{1,0:T(8,128)(2,1)S(1)}, bf16[64,768]{1,0:T(8,128)(2,1)S(1)}, u32[]{:S(2)}, u32[]{:S(2)}) collective-permute-start(bf16[64,768]{1,0:T(8,128)(2,1)S(1)} %get-tuple-element.270), channel_id=1, source_target_pairs={{0,8},{4,12},{8,0},{12,4},{16,24},{20,28},{24,16},{28,20},{1,9},{5... | collective-permute-start | bytes 294920 | tf_op jit(solution)/shard_map/ppermute | solution.py:40
  16.2 11.1 %collective-permute-start.1 = (bf16[64,768]{1,0:T(8,128)(2,1)S(1)}, bf16[64,768]{1,0:T(8,128)(2,1)S(1)}, u32[]{:S(2)}, u32[]{:S(2)}) collective-permute-start(bf16[64,768]{1,0:T(8,128)(2,1)S(1)} %get-tuple-element.271), channel_id=1, source_target_pairs={{0,16},{4,20},{8,24},{12,28},{16,0},{20,4},{24,8},{28,12},{1,17},{... | collective-permute-start | bytes 294920 | tf_op jit(solution)/shard_map/ppermute | solution.py:40
  47.1 12.9 %collective-permute-start.9 = (bf16[256,768]{1,0:T(8,128)(2,1)S(1)}, bf16[256,768]{1,0:T(8,128)(2,1)S(1)}, u32[]{:S(2)}, u32[]{:S(2)}) collective-permute-start(bf16[256,768]{1,0:T(8,128)(2,1)S(1)} %pad_maximum_fusion.11), channel_id=1, source_target_pairs={{0,4},{4,0},{8,12},{12,8},{16,20},{20,16},{24,28},{28,24},{1,5},{5... | collective-permute-start | bytes 1179656 | tf_op jit(solution)/shard_map/ppermute | solution.py:40
  76.0 15.9 %collective-permute-start.21 = (bf16[64,768]{1,0:T(8,128)(2,1)S(1)}, bf16[64,768]{1,0:T(8,128)(2,1)S(1)}, u32[]{:S(2)}, u32[]{:S(2)}) collective-permute-start(bf16[64,768]{1,0:T(8,128)(2,1)S(1)} %get-tuple-element.262), channel_id=1, source_target_pairs={{0,2},{1,3},{2,0},{3,1},{4,6},{5,7},{6,4},{7,5},{8,10},{9,11},{10,... | collective-permute-start | bytes 294920 | tf_op jit(solution)/shard_map/ppermute | solution.py:40
  81.1 13.3 %collective-permute-start.31 = (bf16[64,768]{1,0:T(8,128)(2,1)S(1)}, bf16[64,768]{1,0:T(8,128)(2,1)S(1)}, u32[]{:S(2)}, u32[]{:S(2)}) collective-permute-start(bf16[64,768]{1,0:T(8,128)(2,1)S(1)} %fusion.115), channel_id=1, source_target_pairs={{0,1},{1,0},{2,3},{3,2},{4,5},{5,4},{6,7},{7,6},{8,9},{9,8},{10,11... | collective-permute-start | bytes 294920 | tf_op jit(solution)/shard_map/ppermute | solution.py:40
  81.2 15.3 %collective-permute-start.30 = (bf16[64,768]{1,0:T(8,128)(2,1)S(1)}, bf16[64,768]{1,0:T(8,128)(2,1)S(1)}, u32[]{:S(2)}, u32[]{:S(2)}) collective-permute-start(bf16[64,768]{1,0:T(8,128)(2,1)S(1)} %fusion.115), channel_id=1, source_target_pairs={{0,2},{1,3},{2,0},{3,1},{4,6},{5,7},{6,4},{7,5},{8,10},{9,11},{10,... | collective-permute-start | bytes 294920 | tf_op jit(solution)/shard_map/ppermute | solution.py:40
  83.7 12.7 %collective-permute-start.29 = (bf16[64,768]{1,0:T(8,128)(2,1)S(1)}, bf16[64,768]{1,0:T(8,128)(2,1)S(1)}, u32[]{:S(2)}, u32[]{:S(2)}) collective-permute-start(bf16[64,768]{1,0:T(8,128)(2,1)S(1)} %fusion.115), channel_id=1, source_target_pairs={{0,3},{1,2},{2,1},{3,0},{4,7},{5,6},{6,5},{7,4},{8,11},{9,10},{10,... | collective-permute-start | bytes 294920 | tf_op jit(solution)/shard_map/ppermute | solution.py:40
  121.9 12.6 %collective-permute-start.34 = (bf16[2,32,3072]{2,1,0:T(8,128)(2,1)S(1)}, bf16[2,32,3072]{2,1,0:T(8,128)(2,1)S(1)}, u32[]{:S(2)}, u32[]{:S(2)}) collective-permute-start(bf16[2,32,3072]{2,1,0:T(8,128)(2,1)S(1)} %slice_bitcast_fusion.13), channel_id=1, source_target_pairs={{0,16},{4,20},{8,24},{12,28},{16,0},{20,4},{24,8},{28,12},{1,17},{... | collective-permute-start | bytes 1179656 | tf_op jit(solution)/shard_map/ppermute | solution.py:40
  138.2 13.4 %collective-permute-start.40 = (bf16[2,32,3072]{2,1,0:T(8,128)(2,1)S(1)}, bf16[2,32,3072]{2,1,0:T(8,128)(2,1)S(1)}, u32[]{:S(2)}, u32[]{:S(2)}) collective-permute-start(bf16[2,32,3072]{2,1,0:T(8,128)(2,1)S(1)} %slice_bitcast_fusion.10), channel_id=1, source_target_pairs={{0,8},{4,12},{8,0},{12,4},{16,24},{20,28},{24,16},{28,20},{1,9},{5... | collective-permute-start | bytes 1179656 | tf_op jit(solution)/shard_map/ppermute | solution.py:40
  139.7 12.0 %collective-permute-start.39 = (bf16[2,32,3072]{2,1,0:T(8,128)(2,1)S(1)}, bf16[2,32,3072]{2,1,0:T(8,128)(2,1)S(1)}, u32[]{:S(2)}, u32[]{:S(2)}) collective-permute-start(bf16[2,32,3072]{2,1,0:T(8,128)(2,1)S(1)} %slice_bitcast_fusion.11), channel_id=1, source_target_pairs={{0,16},{4,20},{8,24},{12,28},{16,0},{20,4},{24,8},{28,12},{1,17},{... | collective-permute-start | bytes 1179656 | tf_op jit(solution)/shard_map/ppermute | solution.py:40
  143.3 12.6 %collective-permute-start.38 = (bf16[32,3072]{1,0:T(8,128)(2,1)S(1)}, bf16[32,3072]{1,0:T(8,128)(2,1)S(1)}, u32[]{:S(2)}, u32[]{:S(2)}) collective-permute-start(bf16[32,3072]{1,0:T(8,128)(2,1)S(1)} %get-tuple-element.102), channel_id=1, source_target_pairs={{0,16},{4,20},{8,24},{12,28},{16,0},{20,4},{24,8},{28,12},{1,17},{... | collective-permute-start | bytes 589832 | tf_op jit(solution)/shard_map/ppermute | solution.py:40
  144.9 11.0 %collective-permute-start.41 = (bf16[32,3072]{1,0:T(8,128)(2,1)S(1)}, bf16[32,3072]{1,0:T(8,128)(2,1)S(1)}, u32[]{:S(2)}, u32[]{:S(2)}) collective-permute-start(bf16[32,3072]{1,0:T(8,128)(2,1)S(1)} %get-tuple-element.107.earlier_ref), channel_id=1, source_target_pairs={{0,8},{4,12},{8,0},{12,4},{16,24},{20,28},{24,16},{28,20},{1,9},{5... | collective-permute-start | bytes 589832 | tf_op jit(solution)/shard_map/ppermute | solution.py:40
  155.9 11.7 %collective-permute-start.42 = (bf16[2,32,3072]{2,1,0:T(8,128)(2,1)S(1)}, bf16[2,32,3072]{2,1,0:T(8,128)(2,1)S(1)}, u32[]{:S(2)}, u32[]{:S(2)}) collective-permute-start(bf16[2,32,3072]{2,1,0:T(8,128)(2,1)S(1)} %pad_maximum_fusion.13), channel_id=1, source_target_pairs={{0,8},{4,12},{8,0},{12,4},{16,24},{20,28},{24,16},{28,20},{1,9},{5... | collective-permute-start | bytes 1179656 | tf_op jit(solution)/shard_map/ppermute | solution.py:40
  167.8 11.5 %collective-permute-start.46 = (bf16[2,2,32,6144]{3,2,1,0:T(8,128)(2,1)S(1)}, bf16[2,2,32,6144]{3,2,1,0:T(8,128)(2,1)S(1)}, u32[]{:S(2)}, u32[]{:S(2)}) collective-permute-start(bf16[2,2,32,6144]{3,2,1,0:T(8,128)(2,1)S(1)} %maximum_maximum_fusion), channel_id=1, source_target_pairs={{0,4},{4,0},{8,12},{12,8},{16,20},{20,16},{24,28},{28,24},{1,5},{5... | collective-permute-start | bytes 4718600 | tf_op jit(solution)/shard_map/ppermute | solution.py:40
  231.3 11.9 %collective-permute-start.60 = (bf16[2,32,3072]{2,1,0:T(8,128)(2,1)S(1)}, bf16[2,32,3072]{2,1,0:T(8,128)(2,1)S(1)}, u32[]{:S(2)}, u32[]{:S(2)}) collective-permute-start(bf16[2,32,3072]{2,1,0:T(8,128)(2,1)S(1)} %slice_bitcast_fusion.5), channel_id=1, source_target_pairs={{0,16},{4,20},{8,24},{12,28},{16,0},{20,4},{24,8},{28,12},{1,17},{... | collective-permute-start | bytes 1179656 | tf_op jit(solution)/shard_map/ppermute | solution.py:40
  233.7 12.3 %collective-permute-start.62 = (bf16[2,2,32,6144]{3,2,0,1:T(8,128)(2,1)S(1)}, bf16[2,2,32,6144]{3,2,0,1:T(8,128)(2,1)S(1)}, u32[]{:S(2)}, u32[]{:S(2)}) collective-permute-start(bf16[2,2,32,6144]{3,2,0,1:T(8,128)(2,1)S(1)} %pad_maximum_fusion.8), channel_id=1, source_target_pairs={{0,4},{4,0},{8,12},{12,8},{16,20},{20,16},{24,28},{28,24},{1,5},{5... | collective-permute-start | bytes 4718600 | tf_op jit(solution)/shard_map/ppermute | solution.py:40
  246.7 14.1 %collective-permute-start.66 = (bf16[2,32,3072]{2,1,0:T(8,128)(2,1)S(1)}, bf16[2,32,3072]{2,1,0:T(8,128)(2,1)S(1)}, u32[]{:S(2)}, u32[]{:S(2)}) collective-permute-start(bf16[2,32,3072]{2,1,0:T(8,128)(2,1)S(1)} %slice_bitcast_fusion.2), channel_id=1, source_target_pairs={{0,8},{4,12},{8,0},{12,4},{16,24},{20,28},{24,16},{28,20},{1,9},{5... | collective-permute-start | bytes 1179656 | tf_op jit(solution)/shard_map/ppermute | solution.py:40
  247.3 13.6 %collective-permute-start.65 = (bf16[2,32,3072]{2,1,0:T(8,128)(2,1)S(1)}, bf16[2,32,3072]{2,1,0:T(8,128)(2,1)S(1)}, u32[]{:S(2)}, u32[]{:S(2)}) collective-permute-start(bf16[2,32,3072]{2,1,0:T(8,128)(2,1)S(1)} %slice_bitcast_fusion.3), channel_id=1, source_target_pairs={{0,16},{4,20},{8,24},{12,28},{16,0},{20,4},{24,8},{28,12},{1,17},{... | collective-permute-start | bytes 1179656 | tf_op jit(solution)/shard_map/ppermute | solution.py:40
  253.5 11.6 %collective-permute-start.67 = (bf16[32,3072]{1,0:T(8,128)(2,1)S(1)}, bf16[32,3072]{1,0:T(8,128)(2,1)S(1)}, u32[]{:S(2)}, u32[]{:S(2)}) collective-permute-start(bf16[32,3072]{1,0:T(8,128)(2,1)S(1)} %get-tuple-element.148), channel_id=1, source_target_pairs={{0,8},{4,12},{8,0},{12,4},{16,24},{20,28},{24,16},{28,20},{1,9},{5... | collective-permute-start | bytes 589832 | tf_op jit(solution)/shard_map/ppermute | solution.py:40
  283.5 13.1 %collective-permute-start.75 = (bf16[2,32,3072]{2,1,0:T(8,128)(2,1)S(1)}, bf16[2,32,3072]{2,1,0:T(8,128)(2,1)S(1)}, u32[]{:S(2)}, u32[]{:S(2)}) collective-permute-start(bf16[2,32,3072]{2,1,0:T(8,128)(2,1)S(1)} %pad_maximum_fusion.21), channel_id=1, source_target_pairs={{0,8},{4,12},{8,0},{12,4},{16,24},{20,28},{24,16},{28,20},{1,9},{5... | collective-permute-start | bytes 1179656 | tf_op jit(solution)/shard_map/ppermute | solution.py:40
  284.7 11.9 %collective-permute-start.76 = (bf16[2,32,3072]{2,1,0:T(8,128)(2,1)S(1)}, bf16[2,32,3072]{2,1,0:T(8,128)(2,1)S(1)}, u32[]{:S(2)}, u32[]{:S(2)}) collective-permute-start(bf16[2,32,3072]{2,1,0:T(8,128)(2,1)S(1)} %pad_maximum_fusion.20), channel_id=1, source_target_pairs={{0,16},{4,20},{8,24},{12,28},{16,0},{20,4},{24,8},{28,12},{1,17},{... | collective-permute-start | bytes 1179656 | tf_op jit(solution)/shard_map/ppermute | solution.py:40
  337.8 12.6 %collective-permute-start.87 = (bf16[256,768]{1,0:T(8,128)(2,1)S(1)}, bf16[256,768]{1,0:T(8,128)(2,1)S(1)}, u32[]{:S(2)}, u32[]{:S(2)}) collective-permute-start(bf16[256,768]{1,0:T(8,128)(2,1)S(1)} %pad_maximum_fusion.22), channel_id=1, source_target_pairs={{0,4},{4,0},{8,12},{12,8},{16,20},{20,16},{24,28},{28,24},{1,5},{5... | collective-permute-start | bytes 1179656 | tf_op jit(solution)/shard_map/ppermute | solution.py:40
  357.1 16.5 %collective-permute-start.99 = (bf16[256,384]{1,0:T(8,128)(2,1)S(1)}, bf16[256,384]{1,0:T(8,128)(2,1)S(1)}, u32[]{:S(2)}, u32[]{:S(2)}) collective-permute-start(bf16[256,384]{1,0:T(8,128)(2,1)S(1)} %get-tuple-element.205), channel_id=1, source_target_pairs={{0,2},{1,3},{2,0},{3,1},{4,6},{5,7},{6,4},{7,5},{8,10},{9,11},{10,... | collective-permute-start | bytes 589832 | tf_op jit(solution)/shard_map/ppermute | solution.py:40
  357.1 16.5 %collective-permute-start.100 = (bf16[256,384]{1,0:T(8,128)(2,1)S(1)}, bf16[256,384]{1,0:T(8,128)(2,1)S(1)}, u32[]{:S(2)}, u32[]{:S(2)}) collective-permute-start(bf16[256,384]{1,0:T(8,128)(2,1)S(1)} %get-tuple-element.206), channel_id=1, source_target_pairs={{0,1},{1,0},{2,3},{3,2},{4,5},{5,4},{6,7},{7,6},{8,9},{9,8},{10,11... | collective-permute-start | bytes 589832 | tf_op jit(solution)/shard_map/ppermute | solution.py:40
  (85 other events, 774.1 us)
